TPU v7x, 512 devices: a whole 4x8x8 slice. The times are simulated.
512 devices in a mesh: row: 16 (over x, z_hi, core), col: 32 (over y, z_lo).
Axes of the slice: x: 4, y: 8, z: 8 (z_hi: 2, z_lo: 4; z = z_hi * 4 + z_lo), core: 2. Of those that a mesh axis runs over, the one named last changes fastest.
Arguments:
- points: float32 [8, 4, 1024], P(None, None, 'row'), may hold values from -5 to 5
- frequencies: float32 [8, 8192], replicated, may hold values from -4 to 4
- phases: float32 [8192], replicated, may hold values from -3.140625 to 3.140625
- feature_weights: bfloat16 [8192, 4096], P(None, 'col'), may hold values from -6 to 6
- observed: float32 [4, 1024, 4096], P(None, 'row', 'col'), may hold values from -6 to 6
- factor: float32 [4, 1024, 4096], P(None, 'row', 'col'), as said below
Outputs:
- solution: float32 [4, 1024, 4096], P(None, 'row', 'col')
Inputs may be any that keep to these rules, and one draw needn't show every extreme that they name: `factor`: F(i, j) is zero for j > i, and F(i, i) is lower triangular with its diagonal between 0.5 and 1.5.
All inputs are finite; a program needn't handle non-finite values.
Results may differ from a plain program's by a relative error of at most 0.0017.
Values sent between devices are 32-bit elements; how exact they have to be, the bound alone decides.
No kernel may reach another device: no remote copies, remote signals or barrier semaphores. Data moves between devices by JAX's collectives and lax.ppermute only.
A program may use at most 128 MiB of HBM per device.

v0:
```python
import math

import jax
import jax.numpy as jnp
from jax import lax
from jax.sharding import PartitionSpec as P

highest = lax.Precision.HIGHEST


def product(left, right):
    return jnp.dot(left, right, precision=highest, preferred_element_type=jnp.float32)


def inner_product(left, right):
    return lax.dot_general(
        left, right, (((0,), (0,)), ((), ())), precision=highest, preferred_element_type=jnp.float32
    )


def prior_rows(points, frequencies, phases, feature_weights, block):
    angles = inner_product(points[:, block, :], frequencies) + phases
    features = (math.sqrt(2.0 / frequencies.shape[1]) * jnp.cos(angles)).astype(jnp.bfloat16)
    return jnp.dot(features, feature_weights, preferred_element_type=jnp.float32)


def on_device(points, frequencies, phases, feature_weights, observed, factor):
    blocks = factor.shape[0]
    share = factor.shape[1]
    width = share * lax.axis_size("row")
    col_count = lax.axis_size("col")
    piece_cols = factor.shape[2] // blocks
    pairs = [(block, other) for block in range(blocks) for other in range(block + 1)]
    slabs = {}
    gathered = lax.all_gather(factor, "col", axis=2, tiled=True)
    row_slab = gathered.reshape(blocks, share, col_count, blocks, piece_cols)
    row_slab = row_slab.transpose(0, 1, 3, 2, 4).reshape(blocks, share, blocks * width)
    for block, other in pairs:
        slabs[block, other] = row_slab[block, :, other * width : (other + 1) * width]

    def diagonal(block):
        return slabs[block, block]

    def lower(block, other):
        return slabs[block, other]

    solved_full = []
    solved_mine = []
    for block in range(blocks):
        update = observed[block] - prior_rows(points, frequencies, phases, feature_weights, block)
        for other in range(block):
            update = update - product(lower(block, other), solved_full[other])
        inverse_rows = diagonal(block)
        solved = product(inverse_rows, lax.all_gather(update, "row", axis=0, tiled=True))
        solved_mine.append(solved)
        if block + 1 < blocks:
            solved_full.append(lax.all_gather(solved, "row", axis=0, tiled=True))
    answers = [None] * blocks
    for block in reversed(range(blocks)):
        remain = solved_mine[block]
        if block + 1 < blocks:
            total = jnp.zeros((lax.axis_size("row") * share, remain.shape[1]), jnp.float32)
            for carried_other in range(block + 1, blocks):
                carried_piece = lower(carried_other, block)
                total = total + inner_product(carried_piece, answers[carried_other])
            remain = remain - lax.psum_scatter(total, "row", scatter_dimension=0, tiled=True)
        transposed_piece = diagonal(block)
        answers[block] = lax.psum_scatter(
            inner_product(transposed_piece, remain), "row", scatter_dimension=0, tiled=True
        )
    return jnp.stack(answers)


def solution(mesh):
    in_specs = (
        P(None, None, "row"),
        P(),
        P(),
        P(None, "col"),
        P(None, "row", "col"),
        P(None, "row", "col"),
    )
    out_specs = P(None, "row", "col")
    return jax.shard_map(
        on_device, mesh=mesh, in_specs=in_specs, out_specs=out_specs, check_vma=False
    )
```

profile of v0, /device:TPU:1, one launch (start us, length us, event | category | flops | bytes accessed | tf_op | source)
XLA Modules:
  0.0 1037.6 jit_solution(13667843602924290840)
XLA Ops:
  6.6 1.9 copy.11
  9.5 9.7 fusion.8
  20.4 56.0 %all_gather.24 = f32[1024,128]{1,0:T(8,128)S(1)} all-gather(f32[64,128]{1,0:T(8,128)S(1)} %convolution_subtract_fusion.3), channel_id=1, replica_groups=mesh['row'=16,'col'=32] {'row'}, dimensions={0}, use_global_device_ids=true | all-gather | bytes 557056 | tf_op jit(solution)/shard_map/all_gather | solution.py:54
  76.4 9.7 fusion.9
  86.1 9.7 fusion.10
  95.8 9.4 fusion.11
  106.7 110.5 %all-gather.2.cloned.1.call-done = f32[4,64,4096]{1,2,0:T(8,128)} async-done(((f32[4,64,128]{1,2,0:T(8,128)}), f32[4,64,4096]{1,2,0:T(8,128)}) %all-gather.2.cloned.1.call-update) | async-done | bytes 4194320 | tf_op jit(solution)/shard_map/all_gather | solution.py:35
  217.2 4.4 copy.12
  222.7 36.6 %all_gather.26 = f32[1024,128]{1,0:T(8,128)S(1)} all-gather(f32[64,128]{1,0:T(8,128)S(1)} %convolution_bitcast_fusion.13), channel_id=1, replica_groups=mesh['row'=16,'col'=32] {'row'}, dimensions={0}, use_global_device_ids=true | all-gather | bytes 557056 | tf_op jit(solution)/shard_map/all_gather | solution.py:57
  260.3 28.3 %all_gather.27 = f32[1024,128]{1,0:T(8,128)S(1)} all-gather(f32[64,128]{1,0:T(8,128)S(1)} %fusion.19), channel_id=1, replica_groups=mesh['row'=16,'col'=32] {'row'}, dimensions={0}, use_global_device_ids=true | all-gather | bytes 557056 | tf_op jit(solution)/shard_map/all_gather | solution.py:54
  289.6 30.2 %all_gather.28 = f32[1024,128]{1,0:T(8,128)S(1)} all-gather(f32[64,128]{1,0:T(8,128)S(1)} %convolution_bitcast_fusion.11), channel_id=1, replica_groups=mesh['row'=16,'col'=32] {'row'}, dimensions={0}, use_global_device_ids=true | all-gather | bytes 557056 | tf_op jit(solution)/shard_map/all_gather | solution.py:57
  321.9 28.6 %all_gather.29 = f32[1024,128]{1,0:T(8,128)S(1)} all-gather(f32[64,128]{1,0:T(8,128)S(1)} %fusion.17), channel_id=1, replica_groups=mesh['row'=16,'col'=32] {'row'}, dimensions={0}, use_global_device_ids=true | all-gather | bytes 557056 | tf_op jit(solution)/shard_map/all_gather | solution.py:54
  351.5 29.8 %all_gather.30 = f32[1024,128]{1,0:T(8,128)S(1)} all-gather(f32[64,128]{1,0:T(8,128)S(1)} %convolution_bitcast_fusion.8), channel_id=1, replica_groups=mesh['row'=16,'col'=32] {'row'}, dimensions={0}, use_global_device_ids=true | all-gather | bytes 557056 | tf_op jit(solution)/shard_map/all_gather | solution.py:57
  384.4 28.6 %all_gather.31 = f32[1024,128]{1,0:T(8,128)S(1)} all-gather(f32[64,128]{1,0:T(8,128)S(1)} %fusion.14), channel_id=1, replica_groups=mesh['row'=16,'col'=32] {'row'}, dimensions={0}, use_global_device_ids=true | all-gather | bytes 557056 | tf_op jit(solution)/shard_map/all_gather | solution.py:54
  415.7 94.8 %reduce-scatter.22.cloned.1.call-done = f32[64,128]{1,0:T(8,128)} async-done(((f32[1024,128]{1,0:T(8,128)}), f32[64,128]{1,0:T(8,128)}) %reduce-scatter.22.cloned.1.call-update) | async-done | bytes 32784
  510.6 2.4 convolution_bitcast_fusion.3
  513.1 84.2 %reduce-scatter.16.cloned.1.call-done = f32[64,128]{1,0:T(8,128)} async-done(((f32[1024,128]{1,0:T(8,128)}), f32[64,128]{1,0:T(8,128)}) %reduce-scatter.16.cloned.1.call-update) | async-done | bytes 32784 | tf_op jit(solution)/shard_map/reduce_scatter | solution.py:66
  600.1 83.1 %reduce-scatter.24.cloned.1.call-done = f32[64,128]{1,0:T(8,128)} async-done(((f32[1024,128]{1,0:T(8,128)}), f32[64,128]{1,0:T(8,128)}) %reduce-scatter.24.cloned.1.call-update) | async-done | bytes 32784
  684.9 2.5 fusion.13
  687.4 82.4 %reduce-scatter.18.cloned.1.call-done = f32[64,128]{1,0:T(8,128)} async-done(((f32[1024,128]{1,0:T(8,128)}), f32[64,128]{1,0:T(8,128)}) %reduce-scatter.18.cloned.1.call-update) | async-done | bytes 32784 | tf_op jit(solution)/shard_map/reduce_scatter | solution.py:66
  772.6 83.1 %reduce-scatter.26.cloned.1.call-done = f32[64,128]{1,0:T(8,128)} async-done(((f32[1024,128]{1,0:T(8,128)}), f32[64,128]{1,0:T(8,128)}) %reduce-scatter.26.cloned.1.call-update) | async-done | bytes 32784
  859.0 2.4 fusion.12
  861.6 81.5 %reduce-scatter.20.cloned.1.call-done = f32[64,128]{1,0:T(8,128)} async-done(((f32[1024,128]{1,0:T(8,128)}), f32[64,128]{1,0:T(8,128)}) %reduce-scatter.20.cloned.1.call-update) | async-done | bytes 32784 | tf_op jit(solution)/shard_map/reduce_scatter | solution.py:66
  946.8 82.3 %reduce-scatter.28.cloned.1.call-done = f32[64,128]{1,0:T(8,128)} async-done(((f32[1024,128]{1,0:T(8,128)}), f32[64,128]{1,0:T(8,128)}) %reduce-scatter.28.cloned.1.call-update) | async-done | bytes 32784
  (62 shorter events, 31.7 us)
Async XLA Ops:
  6.5 12.6 %copy-start = (bf16[8192,128]{1,0:T(8,128)(2,1)S(1)}, bf16[8192,128]{1,0:T(8,128)(2,1)}, u32[]{:S(2)}) copy-start(bf16[8192,128]{1,0:T(8,128)(2,1)} %param.9) | copy-start | bytes 6291460
  6.5 89.2 %copy-start.2 = (f32[8,8192]{1,0:T(8,128)S(1)}, f32[8,8192]{1,0:T(8,128)}, u32[]{:S(2)}) copy-start(f32[8,8192]{1,0:T(8,128)} %param.7) | copy-start | bytes 786436
  6.5 89.2 %copy-start.4 = (f32[8192]{0:T(1024)S(1)}, f32[8192]{0:T(1024)}, u32[]{:S(2)}) copy-start(f32[8192]{0:T(1024)} %param.8) | copy-start | bytes 98308
  6.5 98.6 %copy-start.6 = (f32[4,64,128]{2,1,0:T(8,128)S(1)}, f32[4,64,128]{2,1,0:T(8,128)}, u32[]{:S(2)}) copy-start(f32[4,64,128]{2,1,0:T(8,128)} %param.10) | copy-start | bytes 393220
  6.5 210.7 %all-gather.2.cloned.1.call-start = ((), (), s32[]{:S(2)}) async-start(), calls=%async_computation.7 | async-start | bytes 8650752 | tf_op jit(solution)/shard_map/all_gather | solution.py:35
  8.5 502.0 %reduce-scatter.22.cloned.1.call-start = ((), (), s32[]{:S(2)}) async-start(), calls=%async_computation.11 | async-start | bytes 557056
  221.6 192.4 %copy-start.1 = (f32[4,64,4,32,32]{1,4,3,2,0:T(8,128)}, f32[4,64,4,32,32]{1,4,3,2,0:T(8,128)S(1)}, u32[]{:S(2)}) copy-start(f32[4,64,4,32,32]{1,4,3,2,0:T(8,128)S(1)} %copy.12) | copy-start | bytes 12582916
  415.7 181.6 %reduce-scatter.16.cloned.1.call-start = ((), (), s32[]{:S(2)}) async-start(), calls=%async_computation.8 | async-start | bytes 557056 | tf_op jit(solution)/shard_map/reduce_scatter | solution.py:66
  510.6 348.5 %copy-start.3 = (f32[64,128]{1,0:T(8,128)S(1)}, f32[64,128]{1,0:T(8,128)}, u32[]{:S(2)}) copy-start(f32[64,128]{1,0:T(8,128)} %reduce-scatter.22.cloned.1.call-done) | copy-start | bytes 98308
  513.0 170.2 %reduce-scatter.24.cloned.1.call-start = ((), (), s32[]{:S(2)}) async-start(), calls=%async_computation.12 | async-start | bytes 557056
  600.1 169.8 %reduce-scatter.18.cloned.1.call-start = ((), (), s32[]{:S(2)}) async-start(), calls=%async_computation.9 | async-start | bytes 557056 | tf_op jit(solution)/shard_map/reduce_scatter | solution.py:66
  683.3 262.6 %copy-start.5 = (f32[64,128]{1,0:T(8,128)S(1)}, f32[64,128]{1,0:T(8,128)}, u32[]{:S(2)}) copy-start(f32[64,128]{1,0:T(8,128)} %reduce-scatter.24.cloned.1.call-done) | copy-start | bytes 98308
  687.4 168.4 %reduce-scatter.26.cloned.1.call-start = ((), (), s32[]{:S(2)}) async-start(), calls=%async_computation.13 | async-start | bytes 557056
  772.6 170.5 %reduce-scatter.20.cloned.1.call-start = ((), (), s32[]{:S(2)}) async-start(), calls=%async_computation.10 | async-start | bytes 557056 | tf_op jit(solution)/shard_map/reduce_scatter | solution.py:66
  861.5 167.6 %reduce-scatter.28.cloned.1.call-start = ((), (), s32[]{:S(2)}) async-start(), calls=%async_computation.14 | async-start | bytes 557056
Sparse Core Ops, SparseCore 0:
  9.5 207.7 all-gather.1
  415.8 94.7 reduce-scatter.21
  515.9 81.3 reduce-scatter.15
  601.8 81.4 reduce-scatter.23
  688.4 81.3 reduce-scatter.17
  774.3 81.4 reduce-scatter.25
  861.6 81.3 reduce-scatter.19
  947.7 81.3 reduce-scatter.27
where the time goes:
time: 1040 us
  waiting for transfers between devices  702 us (68%)
  blocking collectives  238 us (23%)
  matrix products  69.4 us (7%)
  local copies, waits for them, and re-layouts  13.9 us (1%)
  between operations  13.8 us (1%)
    unnamed x12, waiting for transfers between devices  344 us
    reduce_scatter x3, waiting for transfers between devices, on_device(): lax.psum_scatter(total, 'row', scatter_dimension=0, tiled=True)  248 us
    all_gather x4, blocking collectives, on_device(): lax.all_gather(update, 'row', axis=0, tiled=True)  141 us
    all_gather x1, waiting for transfers between devices, on_device(): gathered = lax.all_gather(factor, 'col', axis=2, tiled=True)  111 us
    all_gather x3, blocking collectives, on_device(): solved_full.append(lax.all_gather(solved, 'row', axis=0, tiled=True))  96.6 us
    dot_general x14, matrix products, inner_product(): lax.dot_general(left, right, (((0,), (0,)), ((), ())), precision=highest,...  56.3 us
  transfers between devices with their start and end apart: 8, of which 8 were waited for; matrix products, arithmetic and copies ran while one was open for 4% of the time, Pallas kernels for 0%

commit v1 on v0

v1 whole, which is shorter than its diff:
```python
import math

import jax
import jax.numpy as jnp
import numpy as np
from jax import lax
from jax.experimental import pallas as pl
from jax.experimental.pallas import tpu as pltpu
from jax.sharding import Mesh
from jax.sharding import PartitionSpec as P

highest = lax.Precision.HIGHEST

SPLIT = {"x": 4, "zh": 2, "core": 2, "y": 8, "zl": 4}
ROW = ("x", "zh", "core")
COL = ("y", "zl")
Z = ("zh", "zl")

HELD = (
    ((0, 0), None, (3, 0)),
    ((1, 1), (1, 0), None),
    ((2, 2), (2, 1), (2, 0)),
    ((3, 3), (3, 2), (3, 1)),
)


def cos_coefficients():
    count = 8
    nodes = 0.125 * (1.0 - np.cos((np.arange(count) + 0.5) * np.pi / count))
    return np.polyfit(nodes * 8.0 - 1.0, np.cos(2.0 * np.pi * np.sqrt(nodes)), count - 1), nodes


def polynomial():
    fitted, _ = cos_coefficients()
    shifted = np.poly1d(fitted)(np.poly1d([8.0, -1.0]))
    return [float(c) for c in shifted.coeffs]


def feature_rows(points, frequencies, phases):
    turn = 1.0 / (2.0 * math.pi)
    rows = points.reshape(points.shape[0], -1)
    turns = lax.dot_general(
        rows, frequencies * turn, (((0,), (0,)), ((), ())), precision=highest, preferred_element_type=jnp.float32
    )
    turns = turns + phases * turn
    part = turns - jnp.round(turns)
    square = part * part
    scale = math.sqrt(2.0 / frequencies.shape[1])
    coefficients = polynomial()
    value = jnp.full_like(square, scale * coefficients[0])
    for c in coefficients[1:]:
        value = value * square + scale * c
    return value.astype(jnp.bfloat16)


def shift(size, step):
    return [(i, (i + step) % size) for i in range(size)]


def ring_gather(unit, axis, size, tasks):
    here = lax.axis_index(axis)
    held = jnp.zeros((size,) + unit.shape, unit.dtype)

    def put(held, piece, step):
        return lax.dynamic_update_slice(held, piece[None], (lax.rem(here + step + size, size),) + (0,) * unit.ndim)

    held = put(held, unit, 0)
    up = down = unit
    done = []
    for step in range(1, size // 2):
        up, down, done = lax.optimization_barrier((up, down, done))
        up = lax.ppermute(up, axis, shift(size, 1))
        down = lax.ppermute(down, axis, shift(size, -1))
        done = tasks[step - 1](done)
        up, down, done = lax.optimization_barrier((up, down, done))
        held = put(held, up, -step)
        held = put(held, down, step)
    half = unit.shape[0] // 2
    first = lax.ppermute(up[:half], axis, shift(size, 1))
    second = lax.ppermute(down[half:], axis, shift(size, -1))
    return put(held, jnp.concatenate([first, second], 0), size // 2), done


def halves(value):
    high = lax.reduce_precision(value, 8, 7)
    return high.astype(jnp.bfloat16), (value - high).astype(jnp.bfloat16)


def times(left, right, contract):
    n = left.shape[0]
    high, low = halves(left)
    dims = (((1,), (contract,)), ((), ()))
    both = lax.dot_general(jnp.concatenate([high, low], 0), right[0], dims, preferred_element_type=jnp.float32)
    rest = lax.dot_general(high, right[1], dims, preferred_element_type=jnp.float32)
    return both[:n] + both[n:] + rest


def spread_lanes(came_ref, unit_ref):
    for place in range(8):
        pieces = [came_ref[4 * place + zl] for zl in range(4)]
        for slot in range(3):
            for rows, base, start in ((slice(0, 48), slot, 0), (slice(16 * slot, 16 * slot + 16), 3, 48)):
                found = None
                for zl in range(4):
                    part = pieces[zl][rows]
                    moved = (zl - base) * 32 % 128
                    part = pltpu.roll(part, moved, 1) if moved else part
                    group = lax.broadcasted_iota(jnp.int32, part.shape, 1) // 32
                    found = part if found is None else jnp.where(group == zl, part, found)
                unit_ref[8 * slot + place, start : start + found.shape[0], :] = found


def lay_out(core_ref, own_ref, other_ref, high_ref, low_ref):
    core = core_ref[0]
    for ref, at in ((own_ref, core), (other_ref, 1 - core)):
        for place in range(ref.shape[1]):
            value = ref[0, place]
            high = value.astype(jnp.bfloat16)
            high_ref[place, at] = high
            low_ref[place, at] = (value - high.astype(jnp.float32)).astype(jnp.bfloat16)


def gather_blocks(factor, tasks):
    blocks, share, lanes = factor.shape
    k = lanes // blocks
    empty = jnp.zeros((share, k), factor.dtype)

    def piece(at):
        return empty if at is None else factor[at[0], :, at[1] * k : (at[1] + 1) * k]

    cut = share * 3 // 4
    send = []
    for slots in HELD:
        parts = [piece(at) for at in slots]
        rest = jnp.concatenate([part[cut:] for part in parts], 0)
        send.append(jnp.concatenate([part[:cut] for part in parts] + [rest], 1))
    send = jnp.broadcast_to(jnp.stack(send)[:, None], (4, 8, cut, 4 * k)).reshape(32, cut, 4 * k)
    came = lax.all_to_all(send, ("x",) + Z, 0, 0, tiled=True)
    unit = pl.pallas_call(
        spread_lanes, out_shape=jax.ShapeDtypeStruct((24, share, 4 * k), jnp.float32), name="spread_lanes"
    )(came)
    along_y, done = ring_gather(unit, "y", 8, tasks)
    other = lax.ppermute(along_y, "core", shift(2, 1))
    core = lax.axis_index("core").reshape(1).astype(jnp.int32)
    taken = pl.BlockSpec((1, 24, share, 4 * k), lambda y, core: (y, 0, 0, 0))
    given = pl.BlockSpec((24, 2, share, 4 * k), lambda y, core: (0, 0, 0, y))
    shape = jax.ShapeDtypeStruct((24, 2, share, 32 * k), jnp.bfloat16)
    both = pl.pallas_call(
        lay_out,
        grid_spec=pltpu.PrefetchScalarGridSpec(
            num_scalar_prefetch=1, grid=(8,), in_specs=[taken, taken], out_specs=[given, given]
        ),
        out_shape=[shape, shape],
        compiler_params=pltpu.CompilerParams(vmem_limit_bytes=24 * 1024 * 1024),
        name="lay_out",
    )(core, along_y, other)
    return [half.reshape(3, 16 * share, 32 * k) for half in both], done


def on_device(points, frequencies, phases, feature_weights, observed, factor):
    blocks, share, width = observed.shape
    samples = width // 4
    size = 16 * share

    def rows(which):
        def task(done):
            found = []
            for block in which:
                features = feature_rows(points[:, block], frequencies, phases)
                prior = jnp.dot(features, feature_weights, preferred_element_type=jnp.float32)
                found.append(observed[block] - prior)
            return done + found

        return task

    def send_rows(done):
        send = jnp.stack(done).reshape(blocks, share, 4, samples).transpose(0, 2, 1, 3)
        send = send.reshape(16, share * samples // 128, 128)
        came = lax.all_to_all(send, ROW, 0, 0, tiled=True)
        return [came.reshape(size, samples).T]

    (high, low), (right,) = gather_blocks(factor, [rows((0, 1)), rows((2, 3)), send_rows])
    diagonal, beside, third = [(high[slot], low[slot]) for slot in range(3)]

    here = lax.axis_index("x")

    def move(value, source, target):
        return lax.ppermute(value, "x", [(source, target)])

    first = times(right, diagonal, 1)
    near = move(first, 0, 1)
    skip = move(first, 0, 2)
    far = move(times(first, third, 1), 0, 3)
    second = times(right - times(near, beside, 1), diagonal, 1)
    near = move(second, 1, 2)
    skip_on = move(second, 1, 3)
    base = right - times(skip, third, 1)
    solved = times(base - times(near, beside, 1), diagonal, 1)
    near = move(solved, 2, 3)
    base = right - far - times(skip_on, third, 1)
    last = times(base - times(near, beside, 1), diagonal, 1)
    mine = jnp.where(here == 0, first, jnp.where(here == 1, second, jnp.where(here == 2, solved, last)))

    fourth = times(mine, diagonal, 0)
    near = move(times(fourth, beside, 0), 3, 2)
    far = move(fourth, 3, 0)
    skip = move(times(fourth, third, 0), 3, 1)
    answer = times(mine - near, diagonal, 0)
    near = move(times(answer, beside, 0), 2, 1)
    skip_on = move(times(answer, third, 0), 2, 0)
    second = times(mine - skip - near, diagonal, 0)
    near = move(times(second, beside, 0), 1, 0)
    base = mine - skip_on - times(far, third, 0)
    first = times(base - near, diagonal, 0)
    result = jnp.where(here == 0, first, jnp.where(here == 1, second, jnp.where(here == 2, answer, fourth)))

    send = result.T.reshape(16, share * samples // 128, 128)
    came = lax.all_to_all(send, ROW, 0, 0, tiled=True)
    came = came.reshape(blocks, 4, share, samples).transpose(0, 2, 1, 3)
    return came.reshape(blocks, share, width)


def solution(mesh):
    fine = Mesh(mesh.devices.reshape(tuple(SPLIT.values())), tuple(SPLIT))
    in_specs = (
        P(None, None, ROW),
        P(),
        P(),
        P(None, COL),
        P(None, ROW, COL),
        P(None, ROW, COL),
    )
    return jax.shard_map(
        on_device, mesh=fine, in_specs=in_specs, out_specs=P(None, ROW, COL), check_vma=False
    )
```

time: 1040 us -> 235 us (0.23)
  waiting for transfers between devices: 702 us -> 57.7 us
  blocking collectives: 238 us -> 18.1 us
  starting transfers between devices: 0.33 us -> 79 us
  matrix products: 69.4 us -> 41.7 us
  between operations: 13.8 us -> 0.85 us
  Pallas kernels: 0 us -> 11.6 us
    unnamed x12 -> x0, waiting for transfers between devices: 344 us -> none
    reduce_scatter x3 -> x0, waiting for transfers between devices: 248 us -> none  [on_device(): lax.psum_scatter(total, 'row', scatter_dimension=0, tiled=True)]
    all_gather x7 -> x0, blocking collectives: 238 us -> none  [the longest x4 141 us: on_device(): lax.all_gather(update, 'row', axis=0, tiled=True)]
    all_gather x1 -> x0, waiting for transfers between devices: 111 us -> none  [on_device(): gathered = lax.all_gather(factor, 'col', axis=2, tiled=True)]
    ppermute x0 -> x21, starting transfers between devices: none -> 45 us  [the longest x12 13.8 us: move(): return lax.ppermute(value, 'x', [(source, target)])]
    ppermute x0 -> x21, waiting for transfers between devices: none -> 43 us  [the longest x12 15.3 us: move(): return lax.ppermute(value, 'x', [(source, target)])]
    all_to_all x0 -> x2, starting transfers between devices: none -> 34 us  [the longest x1 20.3 us: send_rows(): came = lax.all_to_all(send, ROW, 0, 0, tiled=True)]
    dot_general x28 -> x48, matrix products: 69.4 us -> 41.7 us  [the longest x4 14 us: feature_rows(): lax.dot_general(rows, frequencies * turn, (((0,), (0,)), ((), ())), preci...]
  transfers between devices with their start and end apart: 8 -> 23, of which waited for: 8 -> 13; matrix products, arithmetic and copies ran while one was open for 4% -> 21% of each run, Pallas kernels for 0% -> 0%
where the time goes in v1:
time: 235 us; the launch traced here: 234 us
  starting transfers between devices  79 us (34%)
  waiting for transfers between devices  57.7 us (25%)
  matrix products  41.7 us (18%)
  local copies, waits for them, and re-layouts  23.8 us (10%)
  blocking collectives  18.1 us (8%)
  Pallas kernels  11.6 us (5%)
    all_to_all x1, starting transfers between devices, send_rows(): came = lax.all_to_all(send, ROW, 0, 0, tiled=True)  20.3 us
    all_to_all x1, blocking collectives, on_device(): came = lax.all_to_all(send, ROW, 0, 0, tiled=True)  18.1 us
    ppermute x12, waiting for transfers between devices, move(): return lax.ppermute(value, 'x', [(source, target)])  15.3 us
    dot_general x4, matrix products, feature_rows(): lax.dot_general(rows, frequencies * turn, (((0,), (0,)), ((), ())), preci...  14 us
    ppermute x12, starting transfers between devices, move(): return lax.ppermute(value, 'x', [(source, target)])  13.8 us
    all_to_all x1, starting transfers between devices, gather_blocks(): came = lax.all_to_all(send, ('x',) + Z, 0, 0, tiled=True)  13.7 us
    dot_general x20, matrix products, times(): lax.dot_general(jnp.concatenate([high, low], 0), right[0], dims, preferre...  12.4 us
    dot_general x20, matrix products, times(): lax.dot_general(high, right[1], dims, preferred_element_type=jnp.float32)  12.1 us
  transfers between devices with their start and end apart: 23, of which 13 were waited for; matrix products, arithmetic and copies ran while one was open for 21% of the time, Pallas kernels for 0%

profile of v1, /device:TPU:1, one launch (start us, length us, event | category | flops | bytes accessed | tf_op | source)
XLA Modules:
  0.0 234.2 jit_solution(8178749021309397180)
XLA Ops:
  3.3 13.7 %all-to-all-start = ((f32[32,48,128]{2,1,0:T(8,128)}), f32[32,48,128]{2,1,0:T(8,128)S(1)}, u32[]{:S(2)}, u32[]{:S(2)}) async-start(f32[32,48,128]{2,1,0:T(8,128)} %bitcast.247), calls=%async_computation | async-start | bytes 1572864 | tf_op jit(solution)/shard_map/all_to_all | solution.py:138
  17.1 3.0 %add_convert_fusion.2 = bf16[64,8192]{1,0:T(8,128)(2,1)S(1)} fusion(f32[8,64]{1,0:T(8,128)S(1)} %bitcast.257, f32[8192]{0:T(1024)S(1)} %broadcast_multiply_fusion, f32[8,8192]{1,0:T(8,128)S(1)} %copy-done.8), kind=kOutput, calls=%fused_computation.18 | convolution fusion | flops 60358656 | bytes 1345536 | tf_op jit(solution)/shard_map/dot_general | solution.py:42
  20.6 4.0 %add_convert_fusion.3 = bf16[64,8192]{1,0:T(8,128)(2,1)} fusion(f32[8,64]{1,0:T(8,128)S(1)} %bitcast.256, f32[8192]{0:T(1024)S(1)} %broadcast_multiply_fusion, f32[8,8192]{1,0:T(8,128)S(1)} %copy-done.8), kind=kOutput, calls=%fused_computation.19 | convolution fusion | flops 60358656 | bytes 1345536 | tf_op jit(solution)/shard_map/dot_general | solution.py:42
  24.6 4.0 %add_convert_fusion = bf16[64,8192]{1,0:T(8,128)(2,1)} fusion(f32[8,64]{1,0:T(8,128)S(1)} %bitcast.255, f32[8192]{0:T(1024)S(1)} %broadcast_multiply_fusion, f32[8,8192]{1,0:T(8,128)S(1)} %copy-done.8), kind=kOutput, calls=%fused_computation.16 | convolution fusion | flops 60358656 | bytes 1345536 | tf_op jit(solution)/shard_map/dot_general | solution.py:42
  28.7 7.6 %all-to-all-done.came_ref = f32[32,48,128]{2,1,0:T(8,128)S(1)} async-done(((f32[32,48,128]{2,1,0:T(8,128)}), f32[32,48,128]{2,1,0:T(8,128)S(1)}, u32[]{:S(2)}, u32[]{:S(2)}) %all-to-all-start) | async-done | bytes 786464 | tf_op jit(solution)/shard_map/all_to_all | solution.py:138
  39.9 3.3 %collective-permute-start = (f32[24,64,128]{2,1,0:T(8,128)}, f32[24,64,128]{2,1,0:T(8,128)}, u32[]{:S(2)}, u32[]{:S(2)}) collective-permute-start(f32[24,64,128]{2,1,0:T(8,128)} %spread_lanes.1), channel_id=1, source_target_pairs={{0,4},{4,8},{8,12},{12,16},{16,20},{20,24},{24,28},{28,0},{1,5},{5... | collective-permute-start | bytes 2359304 | tf_op jit(solution)/shard_map/ppermute | solution.py:72
  43.2 4.0 %collective-permute-start.1 = (f32[24,64,128]{2,1,0:T(8,128)}, f32[24,64,128]{2,1,0:T(8,128)}, u32[]{:S(2)}, u32[]{:S(2)}) collective-permute-start(f32[24,64,128]{2,1,0:T(8,128)} %spread_lanes.1), channel_id=1, source_target_pairs={{0,28},{4,0},{8,4},{12,8},{16,12},{20,16},{24,20},{28,24},{1,29},{... | collective-permute-start | bytes 2359304 | tf_op jit(solution)/shard_map/ppermute | solution.py:73
  53.0 5.2 %collective-permute-done = f32[24,64,128]{2,1,0:T(8,128)} collective-permute-done((f32[24,64,128]{2,1,0:T(8,128)}, f32[24,64,128]{2,1,0:T(8,128)}, u32[]{:S(2)}, u32[]{:S(2)}) %collective-permute-start) | collective-permute-done | bytes 786464 | tf_op jit(solution)/shard_map/ppermute | solution.py:72
  59.1 3.2 %collective-permute-start.2 = (f32[24,64,128]{2,1,0:T(8,128)}, f32[24,64,128]{2,1,0:T(8,128)S(1)}, u32[]{:S(2)}, u32[]{:S(2)}) collective-permute-start(f32[24,64,128]{2,1,0:T(8,128)} %collective-permute-done), channel_id=1, source_target_pairs={{0,4},{4,8},{8,12},{12,16},{16,20},{20,24},{24,28},{28,0},{1,5},{5... | collective-permute-start | bytes 2359304 | tf_op jit(solution)/shard_map/ppermute | solution.py:72
  62.3 4.0 %collective-permute-start.3 = (f32[24,64,128]{2,1,0:T(8,128)}, f32[24,64,128]{2,1,0:T(8,128)}, u32[]{:S(2)}, u32[]{:S(2)}) collective-permute-start(f32[24,64,128]{2,1,0:T(8,128)} %collective-permute-done.1), channel_id=1, source_target_pairs={{0,28},{4,0},{8,4},{12,8},{16,12},{20,16},{24,20},{28,24},{1,29},{... | collective-permute-start | bytes 2359304 | tf_op jit(solution)/shard_map/ppermute | solution.py:73
  66.9 3.5 %broadcast_in_dim.38 = f32[8,24,64,128]{3,2,1,0:T(8,128)} broadcast(f32[]{:T(128)} %constant.59.clone.1), dimensions={} | broadcast | bytes 6291460 | tf_op jit(solution)/shard_map/broadcast_in_dim | solution.py:62
  73.4 3.0 %collective-permute-done.2 = f32[24,64,128]{2,1,0:T(8,128)S(1)} collective-permute-done((f32[24,64,128]{2,1,0:T(8,128)}, f32[24,64,128]{2,1,0:T(8,128)S(1)}, u32[]{:S(2)}, u32[]{:S(2)}) %collective-permute-start.2) | collective-permute-done | bytes 786464 | tf_op jit(solution)/shard_map/ppermute | solution.py:72
  78.7 4.0 %collective-permute-start.4 = (f32[24,64,128]{2,1,0:T(8,128)S(1)}, f32[24,64,128]{2,1,0:T(8,128)S(1)}, u32[]{:S(2)}, u32[]{:S(2)}) collective-permute-start(f32[24,64,128]{2,1,0:T(8,128)S(1)} %collective-permute-done.2), channel_id=1, source_target_pairs={{0,4},{4,8},{8,12},{12,16},{16,20},{20,24},{24,28},{28,0},{1,5},{5... | collective-permute-start | bytes 2359304 | tf_op jit(solution)/shard_map/ppermute | solution.py:72
  88.8 20.3 %all-to-all-start.1 = ((f32[16,16,128]{2,1,0:T(8,128)}), f32[16,16,128]{2,1,0:T(8,128)S(1)}, u32[]{:S(2)}, u32[]{:S(2)}) async-start(f32[16,16,128]{2,1,0:T(8,128)} %reshape.67), calls=%async_computation.1 | async-start | bytes 262144 | tf_op jit(solution)/shard_map/all_to_all | solution.py:179
  112.1 7.0 %all-to-all-done.1 = f32[16,16,128]{2,1,0:T(8,128)S(1)} async-done(((f32[16,16,128]{2,1,0:T(8,128)}), f32[16,16,128]{2,1,0:T(8,128)S(1)}, u32[]{:S(2)}, u32[]{:S(2)}) %all-to-all-start.1) | async-done | bytes 131104 | tf_op jit(solution)/shard_map/all_to_all | solution.py:179
  119.5 3.1 %collective-permute-start.6 = (f32[12,64,128]{2,1,0:T(8,128)S(1)}, f32[12,64,128]{2,1,0:T(8,128)S(1)}, u32[]{:S(2)}, u32[]{:S(2)}) collective-permute-start(f32[12,64,128]{2,1,0:T(8,128)S(1)} %slice.372), channel_id=1, source_target_pairs={{0,4},{4,8},{8,12},{12,16},{16,20},{20,24},{24,28},{28,0},{1,5},{5... | collective-permute-start | bytes 1179656 | tf_op jit(solution)/shard_map/ppermute | solution.py:79
  122.6 3.4 %collective-permute-start.7 = (f32[12,64,128]{2,1,0:T(8,128)S(1)}, f32[12,64,128]{2,1,0:T(8,128)S(1)}, u32[]{:S(2)}, u32[]{:S(2)}) collective-permute-start(f32[12,64,128]{2,1,0:T(8,128)S(1)} %slice.373), channel_id=1, source_target_pairs={{0,28},{4,0},{8,4},{12,8},{16,12},{20,16},{24,20},{28,24},{1,29},{... | collective-permute-start | bytes 1179656 | tf_op jit(solution)/shard_map/ppermute | solution.py:80
  128.0 4.6 %collective-permute-done.6 = f32[12,64,128]{2,1,0:T(8,128)S(1)} collective-permute-done((f32[12,64,128]{2,1,0:T(8,128)S(1)}, f32[12,64,128]{2,1,0:T(8,128)S(1)}, u32[]{:S(2)}, u32[]{:S(2)}) %collective-permute-start.6) | collective-permute-done | bytes 393248 | tf_op jit(solution)/shard_map/ppermute | solution.py:79
  135.1 3.7 %collective-permute-start.8 = (f32[8,24,64,128]{3,2,1,0:T(8,128)}, f32[8,24,64,128]{3,2,1,0:T(8,128)}, u32[]{:S(2)}, u32[]{:S(2)}) collective-permute-start(f32[8,24,64,128]{3,2,1,0:T(8,128)} %fusion.16.own_ref), channel_id=1, source_target_pairs={{0,32},{32,0},{1,33},{33,1},{2,34},{34,2},{3,35},{35,3},{4,36},{36... | collective-permute-start | bytes 18874376 | tf_op jit(solution)/shard_map/ppermute | solution.py:143
  138.9 10.1 %collective-permute-done.8.other_ref = f32[8,24,64,128]{3,2,1,0:T(8,128)} collective-permute-done((f32[8,24,64,128]{3,2,1,0:T(8,128)}, f32[8,24,64,128]{3,2,1,0:T(8,128)}, u32[]{:S(2)}, u32[]{:S(2)}) %collective-permute-start.8) | collective-permute-done | bytes 6291488 | tf_op jit(solution)/shard_map/ppermute | solution.py:143
  149.0 8.9 %lay_out.1 = (bf16[24,2,64,1024]{3,2,1,0:T(8,128)(2,1)S(1)}, bf16[24,2,64,1024]{3,2,1,0:T(8,128)(2,1)S(1)}) custom-call(s32[1]{0:T(128)} %bitcast.43.core_ref, f32[8,24,64,128]{3,2,1,0:T(8,128)} %fusion.16.own_ref, f32[8,24,64,128]{3,2,1,0:T(8,128)} %collective-permute-done.8.other_ref), custom_call_target="tpu_custom_call" | custom-call | tf_op jit(solution)/shard_map/lay_out/pallas_call | solution.py:148
  200.8 5.2 %collective-permute-done.16 = f32[32,1024]{1,0:T(8,128)S(1)} collective-permute-done((f32[32,1024]{1,0:T(8,128)S(1)}, f32[32,1024]{1,0:T(8,128)S(1)}, u32[]{:S(2)}, u32[]{:S(2)}) %collective-permute-start.16) | collective-permute-done | bytes 131104 | tf_op jit(solution)/shard_map/ppermute | solution.py:188
  206.0 7.0 %collective-permute-done.20 = f32[32,1024]{1,0:T(8,128)S(1)} collective-permute-done((f32[32,1024]{1,0:T(8,128)S(1)}, f32[32,1024]{1,0:T(8,128)S(1)}, u32[]{:S(2)}, u32[]{:S(2)}) %collective-permute-start.20) | collective-permute-done | bytes 131104 | tf_op jit(solution)/shard_map/ppermute | solution.py:188
  214.9 18.1 %all_to_all.15 = f32[16,16,128]{2,1,0:T(8,128)S(1)} all-to-all(f32[16,16,128]{2,1,0:T(8,128)S(1)} %reshape.70), channel_id=1, replica_groups=mesh['x'=4,'zh'=2,'core'=2,'y'=8,'zl'=4] {'x','zh','core'}, dimensions={0} | all-to-all | bytes 262144 | tf_op jit(solution)/shard_map/all_to_all | solution.py:218
  (141 shorter events, 79.3 us)
Async XLA Ops:
  3.3 33.0 %all-to-all-start = ((f32[32,48,128]{2,1,0:T(8,128)}), f32[32,48,128]{2,1,0:T(8,128)S(1)}, u32[]{:S(2)}, u32[]{:S(2)}) async-start(f32[32,48,128]{2,1,0:T(8,128)} %bitcast.247), calls=%async_computation | async-start | bytes 1572864 | tf_op jit(solution)/shard_map/all_to_all | solution.py:138
  39.9 18.3 %collective-permute-start = (f32[24,64,128]{2,1,0:T(8,128)}, f32[24,64,128]{2,1,0:T(8,128)}, u32[]{:S(2)}, u32[]{:S(2)}) collective-permute-start(f32[24,64,128]{2,1,0:T(8,128)} %spread_lanes.1), channel_id=1, source_target_pairs={{0,4},{4,8},{8,12},{12,16},{16,20},{20,24},{24,28},{28,0},{1,5},{5... | collective-permute-start | bytes 2359304 | tf_op jit(solution)/shard_map/ppermute | solution.py:72
  43.2 15.9 %collective-permute-start.1 = (f32[24,64,128]{2,1,0:T(8,128)}, f32[24,64,128]{2,1,0:T(8,128)}, u32[]{:S(2)}, u32[]{:S(2)}) collective-permute-start(f32[24,64,128]{2,1,0:T(8,128)} %spread_lanes.1), channel_id=1, source_target_pairs={{0,28},{4,0},{8,4},{12,8},{16,12},{20,16},{24,20},{28,24},{1,29},{... | collective-permute-start | bytes 2359304 | tf_op jit(solution)/shard_map/ppermute | solution.py:73
  59.1 17.3 %collective-permute-start.2 = (f32[24,64,128]{2,1,0:T(8,128)}, f32[24,64,128]{2,1,0:T(8,128)S(1)}, u32[]{:S(2)}, u32[]{:S(2)}) collective-permute-start(f32[24,64,128]{2,1,0:T(8,128)} %collective-permute-done), channel_id=1, source_target_pairs={{0,4},{4,8},{8,12},{12,16},{16,20},{20,24},{24,28},{28,0},{1,5},{5... | collective-permute-start | bytes 2359304 | tf_op jit(solution)/shard_map/ppermute | solution.py:72
  62.3 16.4 %collective-permute-start.3 = (f32[24,64,128]{2,1,0:T(8,128)}, f32[24,64,128]{2,1,0:T(8,128)}, u32[]{:S(2)}, u32[]{:S(2)}) collective-permute-start(f32[24,64,128]{2,1,0:T(8,128)} %collective-permute-done.1), channel_id=1, source_target_pairs={{0,28},{4,0},{8,4},{12,8},{16,12},{20,16},{24,20},{28,24},{1,29},{... | collective-permute-start | bytes 2359304 | tf_op jit(solution)/shard_map/ppermute | solution.py:73
  78.7 40.7 %collective-permute-start.4 = (f32[24,64,128]{2,1,0:T(8,128)S(1)}, f32[24,64,128]{2,1,0:T(8,128)S(1)}, u32[]{:S(2)}, u32[]{:S(2)}) collective-permute-start(f32[24,64,128]{2,1,0:T(8,128)S(1)} %collective-permute-done.2), channel_id=1, source_target_pairs={{0,4},{4,8},{8,12},{12,16},{16,20},{20,24},{24,28},{28,0},{1,5},{5... | collective-permute-start | bytes 2359304 | tf_op jit(solution)/shard_map/ppermute | solution.py:72
  82.7 36.7 %collective-permute-start.5 = (f32[24,64,128]{2,1,0:T(8,128)}, f32[24,64,128]{2,1,0:T(8,128)S(1)}, u32[]{:S(2)}, u32[]{:S(2)}) collective-permute-start(f32[24,64,128]{2,1,0:T(8,128)} %collective-permute-done.3), channel_id=1, source_target_pairs={{0,28},{4,0},{8,4},{12,8},{16,12},{20,16},{24,20},{28,24},{1,29},{... | collective-permute-start | bytes 2359304 | tf_op jit(solution)/shard_map/ppermute | solution.py:73
  88.8 30.3 %all-to-all-start.1 = ((f32[16,16,128]{2,1,0:T(8,128)}), f32[16,16,128]{2,1,0:T(8,128)S(1)}, u32[]{:S(2)}, u32[]{:S(2)}) async-start(f32[16,16,128]{2,1,0:T(8,128)} %reshape.67), calls=%async_computation.1 | async-start | bytes 262144 | tf_op jit(solution)/shard_map/all_to_all | solution.py:179
  119.5 13.1 %collective-permute-start.6 = (f32[12,64,128]{2,1,0:T(8,128)S(1)}, f32[12,64,128]{2,1,0:T(8,128)S(1)}, u32[]{:S(2)}, u32[]{:S(2)}) collective-permute-start(f32[12,64,128]{2,1,0:T(8,128)S(1)} %slice.372), channel_id=1, source_target_pairs={{0,4},{4,8},{8,12},{12,16},{16,20},{20,24},{24,28},{28,0},{1,5},{5... | collective-permute-start | bytes 1179656 | tf_op jit(solution)/shard_map/ppermute | solution.py:79
  122.6 11.6 %collective-permute-start.7 = (f32[12,64,128]{2,1,0:T(8,128)S(1)}, f32[12,64,128]{2,1,0:T(8,128)S(1)}, u32[]{:S(2)}, u32[]{:S(2)}) collective-permute-start(f32[12,64,128]{2,1,0:T(8,128)S(1)} %slice.373), channel_id=1, source_target_pairs={{0,28},{4,0},{8,4},{12,8},{16,12},{20,16},{24,20},{28,24},{1,29},{... | collective-permute-start | bytes 1179656 | tf_op jit(solution)/shard_map/ppermute | solution.py:80
  135.1 13.9 %collective-permute-start.8 = (f32[8,24,64,128]{3,2,1,0:T(8,128)}, f32[8,24,64,128]{3,2,1,0:T(8,128)}, u32[]{:S(2)}, u32[]{:S(2)}) collective-permute-start(f32[8,24,64,128]{3,2,1,0:T(8,128)} %fusion.16.own_ref), channel_id=1, source_target_pairs={{0,32},{32,0},{1,33},{33,1},{2,34},{34,2},{3,35},{35,3},{4,36},{36... | collective-permute-start | bytes 18874376 | tf_op jit(solution)/shard_map/ppermute | solution.py:143
  161.9 12.5 %collective-permute-start.10 = (f32[32,1024]{1,0:T(8,128)S(1)}, f32[32,1024]{1,0:T(8,128)S(1)}, u32[]{:S(2)}, u32[]{:S(2)}) collective-permute-start(f32[32,1024]{1,0:T(8,128)S(1)} %get-tuple-element.115), channel_id=1, source_target_pairs={{0,256},{1,257},{2,258},{3,259},{4,260},{5,261},{6,262},{7,263},{8... | collective-permute-start | bytes 393224 | tf_op jit(solution)/shard_map/ppermute | solution.py:188
  164.8 5.3 %collective-permute-start.9 = (f32[32,1024]{1,0:T(8,128)S(1)}, f32[32,1024]{1,0:T(8,128)S(1)}, u32[]{:S(2)}, u32[]{:S(2)}) collective-permute-start(f32[32,1024]{1,0:T(8,128)S(1)} %get-tuple-element.115), channel_id=1, source_target_pairs={{0,128},{1,129},{2,130},{3,131},{4,132},{5,133},{6,134},{7,135},{8... | collective-permute-start | bytes 393224 | tf_op jit(solution)/shard_map/ppermute | solution.py:188
  167.5 14.4 %collective-permute-start.12 = (f32[32,1024]{1,0:T(8,128)S(1)}, f32[32,1024]{1,0:T(8,128)S(1)}, u32[]{:S(2)}, u32[]{:S(2)}) collective-permute-start(f32[32,1024]{1,0:T(8,128)S(1)} %convolution_add_fusion.17), channel_id=1, source_target_pairs={{0,384},{1,385},{2,386},{3,387},{4,388},{5,389},{6,390},{7,391},{8... | collective-permute-start | bytes 393224 | tf_op jit(solution)/shard_map/ppermute | solution.py:188
  173.1 2.2 collective-permute-start.11
  173.7 5.9 %collective-permute-start.13 = (f32[32,1024]{1,0:T(8,128)S(1)}, f32[32,1024]{1,0:T(8,128)S(1)}, u32[]{:S(2)}, u32[]{:S(2)}) collective-permute-start(f32[32,1024]{1,0:T(8,128)S(1)} %convolution_add_fusion.21), channel_id=1, source_target_pairs={{128,384},{129,385},{130,386},{131,387},{132,388},{133,389},{134,3... | collective-permute-start | bytes 393224 | tf_op jit(solution)/shard_map/ppermute | solution.py:188
  179.0 2.2 collective-permute-start.14
  186.2 10.8 %collective-permute-start.17 = (f32[32,1024]{1,0:T(8,128)S(1)}, f32[32,1024]{1,0:T(8,128)S(1)}, u32[]{:S(2)}, u32[]{:S(2)}) collective-permute-start(f32[32,1024]{1,0:T(8,128)S(1)} %get-tuple-element.117), channel_id=1, source_target_pairs={{384,0},{385,1},{386,2},{387,3},{388,4},{389,5},{390,6},{391,7},{3... | collective-permute-start | bytes 393224 | tf_op jit(solution)/shard_map/ppermute | solution.py:188
  188.0 1.8 collective-permute-start.15
  189.1 7.9 %collective-permute-start.18 = (f32[32,1024]{1,0:T(8,128)S(1)}, f32[32,1024]{1,0:T(8,128)S(1)}, u32[]{:S(2)}, u32[]{:S(2)}) collective-permute-start(f32[32,1024]{1,0:T(8,128)S(1)} %convolution_add_fusion.8), channel_id=1, source_target_pairs={{384,128},{385,129},{386,130},{387,131},{388,132},{389,133},{390,1... | collective-permute-start | bytes 393224 | tf_op jit(solution)/shard_map/ppermute | solution.py:188
  192.2 13.8 %collective-permute-start.16 = (f32[32,1024]{1,0:T(8,128)S(1)}, f32[32,1024]{1,0:T(8,128)S(1)}, u32[]{:S(2)}, u32[]{:S(2)}) collective-permute-start(f32[32,1024]{1,0:T(8,128)S(1)} %convolution_add_fusion.10), channel_id=1, source_target_pairs={{256,0},{257,1},{258,2},{259,3},{260,4},{261,5},{262,6},{263,7},{2... | collective-permute-start | bytes 393224 | tf_op jit(solution)/shard_map/ppermute | solution.py:188
  194.0 3.0 %collective-permute-start.19 = (f32[32,1024]{1,0:T(8,128)S(1)}, f32[32,1024]{1,0:T(8,128)S(1)}, u32[]{:S(2)}, u32[]{:S(2)}) collective-permute-start(f32[32,1024]{1,0:T(8,128)S(1)} %convolution_add_fusion.7), channel_id=1, source_target_pairs={{256,128},{257,129},{258,130},{259,131},{260,132},{261,133},{262,1... | collective-permute-start | bytes 393224 | tf_op jit(solution)/shard_map/ppermute | solution.py:188
  199.0 14.0 %collective-permute-start.20 = (f32[32,1024]{1,0:T(8,128)S(1)}, f32[32,1024]{1,0:T(8,128)S(1)}, u32[]{:S(2)}, u32[]{:S(2)}) collective-permute-start(f32[32,1024]{1,0:T(8,128)S(1)} %convolution_add_fusion.5), channel_id=1, source_target_pairs={{128,0},{129,1},{130,2},{131,3},{132,4},{133,5},{134,6},{135,7},{1... | collective-permute-start | bytes 393224 | tf_op jit(solution)/shard_map/ppermute | solution.py:188
  214.1 20.2 %copy-start.1 = (bf16[8192,128]{1,0:T(8,128)(2,1)S(1)}, bf16[8192,128]{1,0:T(8,128)(2,1)}, u32[]{:S(2)}) copy-start(bf16[8192,128]{1,0:T(8,128)(2,1)} %param.9) | copy-start | bytes 6291460
  (9 other events, 88.8 us)

commit v2 on v1

--- a/solution.py
+++ b/solution.py
@@ -57,28 +57,32 @@
     return [(i, (i + step) % size) for i in range(size)]
 
 
-def ring_gather(unit, axis, size, tasks):
+def ring_gather(unit, axis, size, parts, beside):
     here = lax.axis_index(axis)
-    held = jnp.zeros((size,) + unit.shape, unit.dtype)
+    rows = unit.shape[0] // parts
+    held = [jnp.zeros((size, rows) + unit.shape[1:], unit.dtype) for _ in range(parts)]
 
     def put(held, piece, step):
-        return lax.dynamic_update_slice(held, piece[None], (lax.rem(here + step + size, size),) + (0,) * unit.ndim)
+        at = (lax.rem(here + step + size, size),) + (0,) * unit.ndim
+        return [
+            lax.dynamic_update_slice(part, piece[None, i * rows : (i + 1) * rows], at) for i, part in enumerate(held)
+        ]
 
     held = put(held, unit, 0)
     up = down = unit
-    done = []
+    result = None
     for step in range(1, size // 2):
-        up, down, done = lax.optimization_barrier((up, down, done))
         up = lax.ppermute(up, axis, shift(size, 1))
         down = lax.ppermute(down, axis, shift(size, -1))
-        done = tasks[step - 1](done)
-        up, down, done = lax.optimization_barrier((up, down, done))
+        if step == 1:
+            result = beside()
+        up, down, result = lax.optimization_barrier((up, down, result))
         held = put(held, up, -step)
         held = put(held, down, step)
     half = unit.shape[0] // 2
     first = lax.ppermute(up[:half], axis, shift(size, 1))
     second = lax.ppermute(down[half:], axis, shift(size, -1))
-    return put(held, jnp.concatenate([first, second], 0), size // 2), done
+    return put(held, jnp.concatenate([first, second], 0), size // 2), result
 
 
 def halves(value):
@@ -120,7 +124,7 @@
             low_ref[place, at] = (value - high.astype(jnp.float32)).astype(jnp.bfloat16)
 
 
-def gather_blocks(factor, tasks):
+def gather_blocks(factor, sides, send_sides):
     blocks, share, lanes = factor.shape
     k = lanes // blocks
     empty = jnp.zeros((share, k), factor.dtype)
@@ -137,24 +141,31 @@
     send = jnp.broadcast_to(jnp.stack(send)[:, None], (4, 8, cut, 4 * k)).reshape(32, cut, 4 * k)
     came = lax.all_to_all(send, ("x",) + Z, 0, 0, tiled=True)
     unit = pl.pallas_call(
-        spread_lanes, out_shape=jax.ShapeDtypeStruct((24, share, 4 * k), jnp.float32), name="spread_lanes"
+        spread_lanes,
+        out_shape=jax.ShapeDtypeStruct((24, share, 4 * k), jnp.float32),
+        compiler_params=pltpu.CompilerParams(vmem_limit_bytes=16 * 1024 * 1024),
+        name="spread_lanes",
     )(came)
-    along_y, done = ring_gather(unit, "y", 8, tasks)
-    other = lax.ppermute(along_y, "core", shift(2, 1))
+    unit, sides = lax.optimization_barrier((unit, sides))
+    held, right = ring_gather(unit, "y", 8, 3, lambda: send_sides(sides))
     core = lax.axis_index("core").reshape(1).astype(jnp.int32)
-    taken = pl.BlockSpec((1, 24, share, 4 * k), lambda y, core: (y, 0, 0, 0))
-    given = pl.BlockSpec((24, 2, share, 4 * k), lambda y, core: (0, 0, 0, y))
-    shape = jax.ShapeDtypeStruct((24, 2, share, 32 * k), jnp.bfloat16)
-    both = pl.pallas_call(
-        lay_out,
-        grid_spec=pltpu.PrefetchScalarGridSpec(
-            num_scalar_prefetch=1, grid=(8,), in_specs=[taken, taken], out_specs=[given, given]
-        ),
-        out_shape=[shape, shape],
-        compiler_params=pltpu.CompilerParams(vmem_limit_bytes=24 * 1024 * 1024),
-        name="lay_out",
-    )(core, along_y, other)
-    return [half.reshape(3, 16 * share, 32 * k) for half in both], done
+    taken = pl.BlockSpec((1, 8, share, 4 * k), lambda y, core: (y, 0, 0, 0))
+    given = pl.BlockSpec((8, 2, share, 4 * k), lambda y, core: (0, 0, 0, y))
+    shape = jax.ShapeDtypeStruct((8, 2, share, 32 * k), jnp.bfloat16)
+    others = [lax.ppermute(part, "core", shift(2, 1)) for part in held]
+    found = []
+    for own, other in zip(held, others):
+        both = pl.pallas_call(
+            lay_out,
+            grid_spec=pltpu.PrefetchScalarGridSpec(
+                num_scalar_prefetch=1, grid=(8,), in_specs=[taken, taken], out_specs=[given, given]
+            ),
+            out_shape=[shape, shape],
+            compiler_params=pltpu.CompilerParams(vmem_limit_bytes=16 * 1024 * 1024),
+            name="lay_out",
+        )(core, own, other)
+        found.append(tuple(half.reshape(16 * share, 32 * k) for half in both))
+    return found, right
 
 
 def on_device(points, frequencies, phases, feature_weights, observed, factor):
@@ -162,25 +173,19 @@
     samples = width // 4
     size = 16 * share
 
-    def rows(which):
-        def task(done):
-            found = []
-            for block in which:
-                features = feature_rows(points[:, block], frequencies, phases)
-                prior = jnp.dot(features, feature_weights, preferred_element_type=jnp.float32)
-                found.append(observed[block] - prior)
-            return done + found
-
-        return task
-
-    def send_rows(done):
-        send = jnp.stack(done).reshape(blocks, share, 4, samples).transpose(0, 2, 1, 3)
-        send = send.reshape(16, share * samples // 128, 128)
+    sides = []
+    for block in range(blocks):
+        features = feature_rows(points[:, block], frequencies, phases)
+        prior = jnp.dot(features, feature_weights, preferred_element_type=jnp.float32)
+        sides.append(observed[block] - prior)
+    send = jnp.stack(sides).reshape(blocks, share, 4, samples).transpose(0, 2, 1, 3)
+    send = send.reshape(16, share * samples // 128, 128)
+
+    def send_sides(send):
         came = lax.all_to_all(send, ROW, 0, 0, tiled=True)
-        return [came.reshape(size, samples).T]
-
-    (high, low), (right,) = gather_blocks(factor, [rows((0, 1)), rows((2, 3)), send_rows])
-    diagonal, beside, third = [(high[slot], low[slot]) for slot in range(3)]
+        return came.reshape(size, samples).T
+
+    (diagonal, beside, third), right = gather_blocks(factor, send, send_sides)
 
     here = lax.axis_index("x")
 

time: 235 us -> 224 us (0.953)
  waiting for transfers between devices: 57.7 us -> 36.6 us
  blocking collectives: 18.1 us -> 36 us
  starting transfers between devices: 79 us -> 65.6 us
  Pallas kernels: 11.6 us -> 16.6 us
  matrix products: 41.7 us -> 38.5 us
  local copies, waits for them, and re-layouts: 23.8 us -> 26.8 us
    all_to_all x1 -> x0, starting transfers between devices: 20.3 us -> none  [send_rows(): came = lax.all_to_all(send, ROW, 0, 0, tiled=True)]
    all_to_all x0 -> x1, blocking collectives: none -> 19.2 us  [send_sides(): came = lax.all_to_all(send, ROW, 0, 0, tiled=True)]
    ppermute x1 -> x3, waiting for transfers between devices: 10.1 us -> 0.01 us  [gather_blocks(): others = [lax.ppermute(part, 'core', shift(2, 1)) for part in held]]
    all_to_all x1 -> x0, waiting for transfers between devices: 7.02 us -> none  [send_rows(): came = lax.all_to_all(send, ROW, 0, 0, tiled=True)]
    pallas_call x1 -> x3, Pallas kernels: 8.9 us -> 15.9 us  [gather_blocks(): pl.pallas_call(lay_out, grid_spec=pltpu.PrefetchScalarGridSpec(num_scalar...]
    ppermute x1 -> x3, starting transfers between devices: 3.74 us -> 10.2 us  [gather_blocks(): others = [lax.ppermute(part, 'core', shift(2, 1)) for part in held]]
    ppermute x3, waiting for transfers between devices: 8.25 us -> 14.4 us  [ring_gather(): up = lax.ppermute(up, axis, shift(size, 1))]
    all_to_all x1, waiting for transfers between devices: 7.64 us -> 2.52 us  [gather_blocks(): came = lax.all_to_all(send, ('x',) + Z, 0, 0, tiled=True)]
  transfers between devices with their start and end apart: 23 -> 24, of which waited for: 13 -> 10; matrix products, arithmetic and copies ran while one was open for 21% -> 24% of each run, Pallas kernels for 0% -> 7%
where the time goes in v2:
time: 224 us; the launch traced here: 223 us
  starting transfers between devices  65.6 us (29%)
  matrix products  38.5 us (17%)
  waiting for transfers between devices  36.6 us (16%)
  blocking collectives  36 us (16%)
  local copies, waits for them, and re-layouts  26.8 us (12%)
  Pallas kernels  16.6 us (7%)
    all_to_all x1, blocking collectives, send_sides(): came = lax.all_to_all(send, ROW, 0, 0, tiled=True)  19.2 us
    all_to_all x1, blocking collectives, on_device(): came = lax.all_to_all(send, ROW, 0, 0, tiled=True)  16.8 us
    pallas_call x3, Pallas kernels, gather_blocks(): pl.pallas_call(lay_out, grid_spec=pltpu.PrefetchScalarGridSpec(num_scalar...  15.9 us
    ppermute x12, starting transfers between devices, move(): return lax.ppermute(value, 'x', [(source, target)])  14.4 us
    ppermute x3, waiting for transfers between devices, ring_gather(): up = lax.ppermute(up, axis, shift(size, 1))  14.4 us
    all_to_all x1, starting transfers between devices, gather_blocks(): came = lax.all_to_all(send, ('x',) + Z, 0, 0, tiled=True)  13.7 us
    dot_general x20, matrix products, times(): lax.dot_general(jnp.concatenate([high, low], 0), right[0], dims, preferre...  12.4 us
    ppermute x3, starting transfers between devices, ring_gather(): down = lax.ppermute(down, axis, shift(size, -1))  12.2 us
  transfers between devices with their start and end apart: 24, of which 10 were waited for; matrix products, arithmetic and copies ran while one was open for 24% of the time, Pallas kernels for 7%

profile of v2, /device:TPU:1, one launch (start us, length us, event | category | flops | bytes accessed | tf_op | source)
XLA Modules:
  0.0 223.0 jit_solution(10027475513992749234)
XLA Ops:
  3.3 13.7 %all-to-all-start = ((f32[32,48,128]{2,1,0:T(8,128)}), f32[32,48,128]{2,1,0:T(8,128)S(1)}, u32[]{:S(2)}, u32[]{:S(2)}) async-start(f32[32,48,128]{2,1,0:T(8,128)} %bitcast.283), calls=%async_computation | async-start | bytes 1572864 | tf_op jit(solution)/shard_map/all_to_all | solution.py:142
  17.1 3.0 %add_convert_fusion.3 = bf16[64,8192]{1,0:T(8,128)(2,1)S(1)} fusion(f32[8,64]{1,0:T(8,128)S(1)} %bitcast.293, f32[8192]{0:T(1024)S(1)} %broadcast_multiply_fusion, f32[8,8192]{1,0:T(8,128)S(1)} %copy-done.6), kind=kOutput, calls=%fused_computation.19 | convolution fusion | flops 60358656 | bytes 1345536 | tf_op jit(solution)/shard_map/dot_general | solution.py:42
  20.1 3.0 %add_convert_fusion.2 = bf16[64,8192]{1,0:T(8,128)(2,1)S(1)} fusion(f32[8,64]{1,0:T(8,128)S(1)} %bitcast.292, f32[8192]{0:T(1024)S(1)} %broadcast_multiply_fusion, f32[8,8192]{1,0:T(8,128)S(1)} %copy-done.6), kind=kOutput, calls=%fused_computation.18 | convolution fusion | flops 60358656 | bytes 1345536 | tf_op jit(solution)/shard_map/dot_general | solution.py:42
  24.4 3.0 %add_convert_fusion.1 = bf16[64,8192]{1,0:T(8,128)(2,1)S(1)} fusion(f32[8,64]{1,0:T(8,128)S(1)} %bitcast.291, f32[8192]{0:T(1024)S(1)} %broadcast_multiply_fusion, f32[8,8192]{1,0:T(8,128)S(1)} %copy-done.6), kind=kOutput, calls=%fused_computation.17 | convolution fusion | flops 60358656 | bytes 1345536 | tf_op jit(solution)/shard_map/dot_general | solution.py:42
  28.0 3.0 %add_convert_fusion = bf16[64,8192]{1,0:T(8,128)(2,1)S(1)} fusion(f32[8,64]{1,0:T(8,128)S(1)} %bitcast.290, f32[8192]{0:T(1024)S(1)} %broadcast_multiply_fusion, f32[8,8192]{1,0:T(8,128)S(1)} %copy-done.6), kind=kOutput, calls=%fused_computation.16 | convolution fusion | flops 60358656 | bytes 1345536 | tf_op jit(solution)/shard_map/dot_general | solution.py:42
  39.1 3.2 %collective-permute-start = (f32[24,64,128]{2,1,0:T(8,128)S(1)}, f32[24,64,128]{2,1,0:T(8,128)}, u32[]{:S(2)}, u32[]{:S(2)}) collective-permute-start(f32[24,64,128]{2,1,0:T(8,128)S(1)} %spread_lanes.1), channel_id=1, source_target_pairs={{0,4},{4,8},{8,12},{12,16},{16,20},{20,24},{24,28},{28,0},{1,5},{5... | collective-permute-start | bytes 2359304 | tf_op jit(solution)/shard_map/ppermute | solution.py:75
  42.3 3.8 %collective-permute-start.1 = (f32[24,64,128]{2,1,0:T(8,128)S(1)}, f32[24,64,128]{2,1,0:T(8,128)}, u32[]{:S(2)}, u32[]{:S(2)}) collective-permute-start(f32[24,64,128]{2,1,0:T(8,128)S(1)} %spread_lanes.1), channel_id=1, source_target_pairs={{0,28},{4,0},{8,4},{12,8},{16,12},{20,16},{24,20},{28,24},{1,29},{... | collective-permute-start | bytes 2359304 | tf_op jit(solution)/shard_map/ppermute | solution.py:76
  46.1 19.2 %all_to_all.15 = f32[16,16,128]{2,1,0:T(8,128)} all-to-all(f32[16,16,128]{2,1,0:T(8,128)S(1)} %reshape.71), channel_id=1, replica_groups=mesh['x'=4,'zh'=2,'core'=2,'y'=8,'zl'=4] {'x','zh','core'}, dimensions={0} | all-to-all | bytes 262144 | tf_op jit(solution)/shard_map/all_to_all | solution.py:185
  68.5 4.6 %collective-permute-start.3 = (f32[24,64,128]{2,1,0:T(8,128)}, f32[24,64,128]{2,1,0:T(8,128)}, u32[]{:S(2)}, u32[]{:S(2)}) collective-permute-start(f32[24,64,128]{2,1,0:T(8,128)} %collective-permute-done.1), channel_id=1, source_target_pairs={{0,28},{4,0},{8,4},{12,8},{16,12},{20,16},{24,20},{28,24},{1,29},{... | collective-permute-start | bytes 2359304 | tf_op jit(solution)/shard_map/ppermute | solution.py:76
  80.2 8.2 %collective-permute-done.2 = f32[24,64,128]{2,1,0:T(8,128)} collective-permute-done((f32[24,64,128]{2,1,0:T(8,128)}, f32[24,64,128]{2,1,0:T(8,128)}, u32[]{:S(2)}, u32[]{:S(2)}) %collective-permute-start.2) | collective-permute-done | bytes 786464 | tf_op jit(solution)/shard_map/ppermute | solution.py:75
  89.3 3.4 %collective-permute-start.4 = (f32[24,64,128]{2,1,0:T(8,128)}, f32[24,64,128]{2,1,0:T(8,128)S(1)}, u32[]{:S(2)}, u32[]{:S(2)}) collective-permute-start(f32[24,64,128]{2,1,0:T(8,128)} %collective-permute-done.2), channel_id=1, source_target_pairs={{0,4},{4,8},{8,12},{12,16},{16,20},{20,24},{24,28},{28,0},{1,5},{5... | collective-permute-start | bytes 2359304 | tf_op jit(solution)/shard_map/ppermute | solution.py:75
  92.7 3.8 %collective-permute-start.5 = (f32[24,64,128]{2,1,0:T(8,128)}, f32[24,64,128]{2,1,0:T(8,128)S(1)}, u32[]{:S(2)}, u32[]{:S(2)}) collective-permute-start(f32[24,64,128]{2,1,0:T(8,128)} %collective-permute-done.3), channel_id=1, source_target_pairs={{0,28},{4,0},{8,4},{12,8},{16,12},{20,16},{24,20},{28,24},{1,29},{... | collective-permute-start | bytes 2359304 | tf_op jit(solution)/shard_map/ppermute | solution.py:76
  104.6 6.2 %collective-permute-done.4 = f32[24,64,128]{2,1,0:T(8,128)S(1)} collective-permute-done((f32[24,64,128]{2,1,0:T(8,128)}, f32[24,64,128]{2,1,0:T(8,128)S(1)}, u32[]{:S(2)}, u32[]{:S(2)}) %collective-permute-start.4) | collective-permute-done | bytes 786464 | tf_op jit(solution)/shard_map/ppermute | solution.py:75
  110.8 3.1 %collective-permute-done.5 = f32[24,64,128]{2,1,0:T(8,128)S(1)} collective-permute-done((f32[24,64,128]{2,1,0:T(8,128)}, f32[24,64,128]{2,1,0:T(8,128)S(1)}, u32[]{:S(2)}, u32[]{:S(2)}) %collective-permute-start.5) | collective-permute-done | bytes 786464 | tf_op jit(solution)/shard_map/ppermute | solution.py:76
  113.9 3.9 %collective-permute-start.6 = (f32[12,64,128]{2,1,0:T(8,128)S(1)}, f32[12,64,128]{2,1,0:T(8,128)S(1)}, u32[]{:S(2)}, u32[]{:S(2)}) collective-permute-start(f32[12,64,128]{2,1,0:T(8,128)S(1)} %slice.427), channel_id=1, source_target_pairs={{0,4},{4,8},{8,12},{12,16},{16,20},{20,24},{24,28},{28,0},{1,5},{5... | collective-permute-start | bytes 1179656 | tf_op jit(solution)/shard_map/ppermute | solution.py:83
  117.9 2.6 %collective-permute-start.9 = (f32[12,64,128]{2,1,0:T(8,128)S(1)}, f32[12,64,128]{2,1,0:T(8,128)S(1)}, u32[]{:S(2)}, u32[]{:S(2)}) collective-permute-start(f32[12,64,128]{2,1,0:T(8,128)S(1)} %slice.438), channel_id=1, source_target_pairs={{0,28},{4,0},{8,4},{12,8},{16,12},{20,16},{24,20},{28,24},{1,29},{... | collective-permute-start | bytes 1179656 | tf_op jit(solution)/shard_map/ppermute | solution.py:84
  122.3 2.9 %collective-permute-done.6 = f32[12,64,128]{2,1,0:T(8,128)S(1)} collective-permute-done((f32[12,64,128]{2,1,0:T(8,128)S(1)}, f32[12,64,128]{2,1,0:T(8,128)S(1)}, u32[]{:S(2)}, u32[]{:S(2)}) %collective-permute-start.6) | collective-permute-done | bytes 393248 | tf_op jit(solution)/shard_map/ppermute | solution.py:83
  128.2 5.9 %collective-permute-start.7 = (f32[8,8,64,128]{3,2,1,0:T(8,128)}, f32[8,8,64,128]{3,2,1,0:T(8,128)}, u32[]{:S(2)}, u32[]{:S(2)}) collective-permute-start(f32[8,8,64,128]{3,2,1,0:T(8,128)} %get-tuple-element.65.own_ref), channel_id=1, source_target_pairs={{0,32},{32,0},{1,33},{33,1},{2,34},{34,2},{3,35},{35,3},{4,36},{36... | collective-permute-start | bytes 6291464 | tf_op jit(solution)/shard_map/ppermute | solution.py:155
  138.5 5.3 %lay_out.3 = (bf16[8,2,64,1024]{3,2,1,0:T(8,128)(2,1)S(1)}, bf16[8,2,64,1024]{3,2,1,0:T(8,128)(2,1)S(1)}) custom-call(s32[1]{0:T(128)} %bitcast.43.core_ref, f32[8,8,64,128]{3,2,1,0:T(8,128)} %get-tuple-element.65.own_ref, f32[8,8,64,128]{3,2,1,0:T(8,128)} %collective-permute-done.7.other_ref), custom_call_target="tpu_custom_call" | custom-call | tf_op jit(solution)/shard_map/lay_out/pallas_call | solution.py:158
  145.3 3.8 %collective-permute-start.11 = (f32[32,1024]{1,0:T(8,128)S(1)}, f32[32,1024]{1,0:T(8,128)S(1)}, u32[]{:S(2)}, u32[]{:S(2)}) collective-permute-start(f32[32,1024]{1,0:T(8,128)S(1)} %get-tuple-element.122), channel_id=1, source_target_pairs={{0,256},{1,257},{2,258},{3,259},{4,260},{5,261},{6,262},{7,263},{8... | collective-permute-start | bytes 393224 | tf_op jit(solution)/shard_map/ppermute | solution.py:193
  150.4 5.3 %lay_out.5 = (bf16[8,2,64,1024]{3,2,1,0:T(8,128)(2,1)S(1)}, bf16[8,2,64,1024]{3,2,1,0:T(8,128)(2,1)S(1)}) custom-call(s32[1]{0:T(128)} %bitcast.43.core_ref, f32[8,8,64,128]{3,2,1,0:T(8,128)} %get-tuple-element.63.own_ref, f32[8,8,64,128]{3,2,1,0:T(8,128)} %collective-permute-done.12.other_ref), custom_call_target="tpu_custom_call" | custom-call | tf_op jit(solution)/shard_map/lay_out/pallas_call | solution.py:158
  158.5 5.3 %lay_out.4 = (bf16[8,2,64,1024]{3,2,1,0:T(8,128)(2,1)S(1)}, bf16[8,2,64,1024]{3,2,1,0:T(8,128)(2,1)S(1)}) custom-call(s32[1]{0:T(128)} %bitcast.43.core_ref, f32[8,8,64,128]{3,2,1,0:T(8,128)} %get-tuple-element.64.own_ref, f32[8,8,64,128]{3,2,1,0:T(8,128)} %collective-permute-done.10.other_ref), custom_call_target="tpu_custom_call" | custom-call | tf_op jit(solution)/shard_map/lay_out/pallas_call | solution.py:158
  196.6 7.0 %collective-permute-done.22 = f32[32,1024]{1,0:T(8,128)S(1)} collective-permute-done((f32[32,1024]{1,0:T(8,128)S(1)}, f32[32,1024]{1,0:T(8,128)S(1)}, u32[]{:S(2)}, u32[]{:S(2)}) %collective-permute-start.22) | collective-permute-done | bytes 131104 | tf_op jit(solution)/shard_map/ppermute | solution.py:193
  205.1 16.8 %all_to_all.16 = f32[16,16,128]{2,1,0:T(8,128)S(1)} all-to-all(f32[16,16,128]{2,1,0:T(8,128)S(1)} %reshape.80), channel_id=1, replica_groups=mesh['x'=4,'zh'=2,'core'=2,'y'=8,'zl'=4] {'x','zh','core'}, dimensions={0} | all-to-all | bytes 262144 | tf_op jit(solution)/shard_map/all_to_all | solution.py:223
  (143 shorter events, 82.2 us)
Async XLA Ops:
  3.3 33.0 %all-to-all-start = ((f32[32,48,128]{2,1,0:T(8,128)}), f32[32,48,128]{2,1,0:T(8,128)S(1)}, u32[]{:S(2)}, u32[]{:S(2)}) async-start(f32[32,48,128]{2,1,0:T(8,128)} %bitcast.283), calls=%async_computation | async-start | bytes 1572864 | tf_op jit(solution)/shard_map/all_to_all | solution.py:142
  39.1 27.5 %collective-permute-start = (f32[24,64,128]{2,1,0:T(8,128)S(1)}, f32[24,64,128]{2,1,0:T(8,128)}, u32[]{:S(2)}, u32[]{:S(2)}) collective-permute-start(f32[24,64,128]{2,1,0:T(8,128)S(1)} %spread_lanes.1), channel_id=1, source_target_pairs={{0,4},{4,8},{8,12},{12,16},{16,20},{20,24},{24,28},{28,0},{1,5},{5... | collective-permute-start | bytes 2359304 | tf_op jit(solution)/shard_map/ppermute | solution.py:75
  42.3 24.3 %collective-permute-start.1 = (f32[24,64,128]{2,1,0:T(8,128)S(1)}, f32[24,64,128]{2,1,0:T(8,128)}, u32[]{:S(2)}, u32[]{:S(2)}) collective-permute-start(f32[24,64,128]{2,1,0:T(8,128)S(1)} %spread_lanes.1), channel_id=1, source_target_pairs={{0,28},{4,0},{8,4},{12,8},{16,12},{20,16},{24,20},{28,24},{1,29},{... | collective-permute-start | bytes 2359304 | tf_op jit(solution)/shard_map/ppermute | solution.py:76
  66.6 21.8 %collective-permute-start.2 = (f32[24,64,128]{2,1,0:T(8,128)}, f32[24,64,128]{2,1,0:T(8,128)}, u32[]{:S(2)}, u32[]{:S(2)}) collective-permute-start(f32[24,64,128]{2,1,0:T(8,128)} %collective-permute-done), channel_id=1, source_target_pairs={{0,4},{4,8},{8,12},{12,16},{16,20},{20,24},{24,28},{28,0},{1,5},{5... | collective-permute-start | bytes 2359304 | tf_op jit(solution)/shard_map/ppermute | solution.py:75
  68.5 20.8 %collective-permute-start.3 = (f32[24,64,128]{2,1,0:T(8,128)}, f32[24,64,128]{2,1,0:T(8,128)}, u32[]{:S(2)}, u32[]{:S(2)}) collective-permute-start(f32[24,64,128]{2,1,0:T(8,128)} %collective-permute-done.1), channel_id=1, source_target_pairs={{0,28},{4,0},{8,4},{12,8},{16,12},{20,16},{24,20},{28,24},{1,29},{... | collective-permute-start | bytes 2359304 | tf_op jit(solution)/shard_map/ppermute | solution.py:76
  89.3 21.5 %collective-permute-start.4 = (f32[24,64,128]{2,1,0:T(8,128)}, f32[24,64,128]{2,1,0:T(8,128)S(1)}, u32[]{:S(2)}, u32[]{:S(2)}) collective-permute-start(f32[24,64,128]{2,1,0:T(8,128)} %collective-permute-done.2), channel_id=1, source_target_pairs={{0,4},{4,8},{8,12},{12,16},{16,20},{20,24},{24,28},{28,0},{1,5},{5... | collective-permute-start | bytes 2359304 | tf_op jit(solution)/shard_map/ppermute | solution.py:75
  92.7 21.2 %collective-permute-start.5 = (f32[24,64,128]{2,1,0:T(8,128)}, f32[24,64,128]{2,1,0:T(8,128)S(1)}, u32[]{:S(2)}, u32[]{:S(2)}) collective-permute-start(f32[24,64,128]{2,1,0:T(8,128)} %collective-permute-done.3), channel_id=1, source_target_pairs={{0,28},{4,0},{8,4},{12,8},{16,12},{20,16},{24,20},{28,24},{1,29},{... | collective-permute-start | bytes 2359304 | tf_op jit(solution)/shard_map/ppermute | solution.py:76
  113.9 11.3 %collective-permute-start.6 = (f32[12,64,128]{2,1,0:T(8,128)S(1)}, f32[12,64,128]{2,1,0:T(8,128)S(1)}, u32[]{:S(2)}, u32[]{:S(2)}) collective-permute-start(f32[12,64,128]{2,1,0:T(8,128)S(1)} %slice.427), channel_id=1, source_target_pairs={{0,4},{4,8},{8,12},{12,16},{16,20},{20,24},{24,28},{28,0},{1,5},{5... | collective-permute-start | bytes 1179656 | tf_op jit(solution)/shard_map/ppermute | solution.py:83
  117.9 9.5 %collective-permute-start.9 = (f32[12,64,128]{2,1,0:T(8,128)S(1)}, f32[12,64,128]{2,1,0:T(8,128)S(1)}, u32[]{:S(2)}, u32[]{:S(2)}) collective-permute-start(f32[12,64,128]{2,1,0:T(8,128)S(1)} %slice.438), channel_id=1, source_target_pairs={{0,28},{4,0},{8,4},{12,8},{16,12},{20,16},{24,20},{28,24},{1,29},{... | collective-permute-start | bytes 1179656 | tf_op jit(solution)/shard_map/ppermute | solution.py:84
  128.2 10.3 %collective-permute-start.7 = (f32[8,8,64,128]{3,2,1,0:T(8,128)}, f32[8,8,64,128]{3,2,1,0:T(8,128)}, u32[]{:S(2)}, u32[]{:S(2)}) collective-permute-start(f32[8,8,64,128]{3,2,1,0:T(8,128)} %get-tuple-element.65.own_ref), channel_id=1, source_target_pairs={{0,32},{32,0},{1,33},{33,1},{2,34},{34,2},{3,35},{35,3},{4,36},{36... | collective-permute-start | bytes 6291464 | tf_op jit(solution)/shard_map/ppermute | solution.py:155
  134.1 16.3 %collective-permute-start.12 = (f32[8,8,64,128]{3,2,1,0:T(8,128)}, f32[8,8,64,128]{3,2,1,0:T(8,128)}, u32[]{:S(2)}, u32[]{:S(2)}) collective-permute-start(f32[8,8,64,128]{3,2,1,0:T(8,128)} %get-tuple-element.63.own_ref), channel_id=1, source_target_pairs={{0,32},{32,0},{1,33},{33,1},{2,34},{34,2},{3,35},{35,3},{4,36},{36... | collective-permute-start | bytes 6291464 | tf_op jit(solution)/shard_map/ppermute | solution.py:155
  136.0 22.4 %collective-permute-start.10 = (f32[8,8,64,128]{3,2,1,0:T(8,128)}, f32[8,8,64,128]{3,2,1,0:T(8,128)}, u32[]{:S(2)}, u32[]{:S(2)}) collective-permute-start(f32[8,8,64,128]{3,2,1,0:T(8,128)} %get-tuple-element.64.own_ref), channel_id=1, source_target_pairs={{0,32},{32,0},{1,33},{33,1},{2,34},{34,2},{3,35},{35,3},{4,36},{36... | collective-permute-start | bytes 6291464 | tf_op jit(solution)/shard_map/ppermute | solution.py:155
  145.3 22.9 %collective-permute-start.11 = (f32[32,1024]{1,0:T(8,128)S(1)}, f32[32,1024]{1,0:T(8,128)S(1)}, u32[]{:S(2)}, u32[]{:S(2)}) collective-permute-start(f32[32,1024]{1,0:T(8,128)S(1)} %get-tuple-element.122), channel_id=1, source_target_pairs={{0,256},{1,257},{2,258},{3,259},{4,260},{5,261},{6,262},{7,263},{8... | collective-permute-start | bytes 393224 | tf_op jit(solution)/shard_map/ppermute | solution.py:193
  149.1 14.7 %collective-permute-start.8 = (f32[32,1024]{1,0:T(8,128)S(1)}, f32[32,1024]{1,0:T(8,128)S(1)}, u32[]{:S(2)}, u32[]{:S(2)}) collective-permute-start(f32[32,1024]{1,0:T(8,128)S(1)} %get-tuple-element.122), channel_id=1, source_target_pairs={{0,128},{1,129},{2,130},{3,131},{4,132},{5,133},{6,134},{7,135},{8... | collective-permute-start | bytes 393224 | tf_op jit(solution)/shard_map/ppermute | solution.py:193
  157.2 18.8 %collective-permute-start.14 = (f32[32,1024]{1,0:T(8,128)S(1)}, f32[32,1024]{1,0:T(8,128)S(1)}, u32[]{:S(2)}, u32[]{:S(2)}) collective-permute-start(f32[32,1024]{1,0:T(8,128)S(1)} %convolution_add_fusion.17), channel_id=1, source_target_pairs={{0,384},{1,385},{2,386},{3,387},{4,388},{5,389},{6,390},{7,391},{8... | collective-permute-start | bytes 393224 | tf_op jit(solution)/shard_map/ppermute | solution.py:193
  166.8 2.2 collective-permute-start.13
  167.5 6.1 %collective-permute-start.15 = (f32[32,1024]{1,0:T(8,128)S(1)}, f32[32,1024]{1,0:T(8,128)S(1)}, u32[]{:S(2)}, u32[]{:S(2)}) collective-permute-start(f32[32,1024]{1,0:T(8,128)S(1)} %convolution_add_fusion.21), channel_id=1, source_target_pairs={{128,384},{129,385},{130,386},{131,387},{132,388},{133,389},{134,3... | collective-permute-start | bytes 393224 | tf_op jit(solution)/shard_map/ppermute | solution.py:193
  172.7 2.4 %collective-permute-start.16 = (f32[32,1024]{1,0:T(8,128)S(1)}, f32[32,1024]{1,0:T(8,128)S(1)}, u32[]{:S(2)}, u32[]{:S(2)}) collective-permute-start(f32[32,1024]{1,0:T(8,128)S(1)} %convolution_add_fusion.18), channel_id=1, source_target_pairs={{256,384},{257,385},{258,386},{259,387},{260,388},{261,389},{262,3... | collective-permute-start | bytes 393224 | tf_op jit(solution)/shard_map/ppermute | solution.py:193
  180.7 3.1 %collective-permute-start.17 = (f32[32,1024]{1,0:T(8,128)S(1)}, f32[32,1024]{1,0:T(8,128)S(1)}, u32[]{:S(2)}, u32[]{:S(2)}) collective-permute-start(f32[32,1024]{1,0:T(8,128)S(1)} %convolution_add_fusion.12), channel_id=1, source_target_pairs={{384,256},{385,257},{386,258},{387,259},{388,260},{389,261},{390,2... | collective-permute-start | bytes 393224 | tf_op jit(solution)/shard_map/ppermute | solution.py:193
  181.4 9.3 %collective-permute-start.19 = (f32[32,1024]{1,0:T(8,128)S(1)}, f32[32,1024]{1,0:T(8,128)S(1)}, u32[]{:S(2)}, u32[]{:S(2)}) collective-permute-start(f32[32,1024]{1,0:T(8,128)S(1)} %get-tuple-element.124), channel_id=1, source_target_pairs={{384,0},{385,1},{386,2},{387,3},{388,4},{389,5},{390,6},{391,7},{3... | collective-permute-start | bytes 393224 | tf_op jit(solution)/shard_map/ppermute | solution.py:193
  183.1 8.0 %collective-permute-start.20 = (f32[32,1024]{1,0:T(8,128)S(1)}, f32[32,1024]{1,0:T(8,128)S(1)}, u32[]{:S(2)}, u32[]{:S(2)}) collective-permute-start(f32[32,1024]{1,0:T(8,128)S(1)} %convolution_add_fusion.8), channel_id=1, source_target_pairs={{384,128},{385,129},{386,130},{387,131},{388,132},{389,133},{390,1... | collective-permute-start | bytes 393224 | tf_op jit(solution)/shard_map/ppermute | solution.py:193
  186.3 10.3 %collective-permute-start.18 = (f32[32,1024]{1,0:T(8,128)S(1)}, f32[32,1024]{1,0:T(8,128)S(1)}, u32[]{:S(2)}, u32[]{:S(2)}) collective-permute-start(f32[32,1024]{1,0:T(8,128)S(1)} %convolution_add_fusion.10), channel_id=1, source_target_pairs={{256,0},{257,1},{258,2},{259,3},{260,4},{261,5},{262,6},{263,7},{2... | collective-permute-start | bytes 393224 | tf_op jit(solution)/shard_map/ppermute | solution.py:193
  188.1 3.1 %collective-permute-start.21 = (f32[32,1024]{1,0:T(8,128)S(1)}, f32[32,1024]{1,0:T(8,128)S(1)}, u32[]{:S(2)}, u32[]{:S(2)}) collective-permute-start(f32[32,1024]{1,0:T(8,128)S(1)} %convolution_add_fusion.7), channel_id=1, source_target_pairs={{256,128},{257,129},{258,130},{259,131},{260,132},{261,133},{262,1... | collective-permute-start | bytes 393224 | tf_op jit(solution)/shard_map/ppermute | solution.py:193
  193.1 10.5 %collective-permute-start.22 = (f32[32,1024]{1,0:T(8,128)S(1)}, f32[32,1024]{1,0:T(8,128)S(1)}, u32[]{:S(2)}, u32[]{:S(2)}) collective-permute-start(f32[32,1024]{1,0:T(8,128)S(1)} %convolution_add_fusion.5), channel_id=1, source_target_pairs={{128,0},{129,1},{130,2},{131,3},{132,4},{133,5},{134,6},{135,7},{1... | collective-permute-start | bytes 393224 | tf_op jit(solution)/shard_map/ppermute | solution.py:193
  (7 other events, 79.5 us)

commit v3 on v2

--- a/solution.py
+++ b/solution.py
@@ -76,7 +76,7 @@
         down = lax.ppermute(down, axis, shift(size, -1))
         if step == 1:
             result = beside()
-        up, down, result = lax.optimization_barrier((up, down, result))
+            down, result = lax.optimization_barrier((down, result))
         held = put(held, up, -step)
         held = put(held, down, step)
     half = unit.shape[0] // 2
@@ -116,12 +116,17 @@
 
 def lay_out(core_ref, own_ref, other_ref, high_ref, low_ref):
     core = core_ref[0]
-    for ref, at in ((own_ref, core), (other_ref, 1 - core)):
-        for place in range(ref.shape[1]):
-            value = ref[0, place]
-            high = value.astype(jnp.bfloat16)
-            high_ref[place, at] = high
-            low_ref[place, at] = (value - high.astype(jnp.float32)).astype(jnp.bfloat16)
+
+    def one(place, carry):
+        for ref, at in ((own_ref, core), (other_ref, 1 - core)):
+            for y in range(ref.shape[0]):
+                value = ref[y, place]
+                high = value.astype(jnp.bfloat16)
+                high_ref[place, at, :, 128 * y : 128 * y + 128] = high
+                low_ref[place, at, :, 128 * y : 128 * y + 128] = (value - high.astype(jnp.float32)).astype(jnp.bfloat16)
+        return carry
+
+    lax.fori_loop(0, own_ref.shape[1], one, 0)
 
 
 def gather_blocks(factor, sides, send_sides):
@@ -149,17 +154,17 @@
     unit, sides = lax.optimization_barrier((unit, sides))
     held, right = ring_gather(unit, "y", 8, 3, lambda: send_sides(sides))
     core = lax.axis_index("core").reshape(1).astype(jnp.int32)
-    taken = pl.BlockSpec((1, 8, share, 4 * k), lambda y, core: (y, 0, 0, 0))
-    given = pl.BlockSpec((8, 2, share, 4 * k), lambda y, core: (0, 0, 0, y))
+    whole = pl.BlockSpec(memory_space=pltpu.VMEM)
     shape = jax.ShapeDtypeStruct((8, 2, share, 32 * k), jnp.bfloat16)
     others = [lax.ppermute(part, "core", shift(2, 1)) for part in held]
     found = []
     for own, other in zip(held, others):
+        if found:
+            other, found[-1] = lax.optimization_barrier((other, found[-1]))
         both = pl.pallas_call(
             lay_out,
-            grid_spec=pltpu.PrefetchScalarGridSpec(
-                num_scalar_prefetch=1, grid=(8,), in_specs=[taken, taken], out_specs=[given, given]
-            ),
+            in_specs=[pl.BlockSpec(memory_space=pltpu.SMEM), whole, whole],
+            out_specs=[whole, whole],
             out_shape=[shape, shape],
             compiler_params=pltpu.CompilerParams(vmem_limit_bytes=16 * 1024 * 1024),
             name="lay_out",

time: 224 us -> 217 us (0.969)
  Pallas kernels: 16.6 us -> 9.8 us
  starting transfers between devices: 65.6 us -> 63.1 us
    pallas_call x3, Pallas kernels: 15.9 us -> 9.13 us  [gather_blocks(): pl.pallas_call(lay_out, in_specs=[pl.BlockSpec(memory_space=pltpu.SMEM),...]
    ppermute x3, waiting for transfers between devices: 14.4 us -> 8.45 us  [ring_gather(): up = lax.ppermute(up, axis, shift(size, 1))]
    ppermute x3, waiting for transfers between devices: 3.95 us -> 7.45 us  [ring_gather(): down = lax.ppermute(down, axis, shift(size, -1))]
    ppermute x3, starting transfers between devices: 8.52 us -> 5.75 us  [ring_gather(): up = lax.ppermute(up, axis, shift(size, 1))]
    ppermute x1, starting transfers between devices: 2.56 us -> 5.21 us  [ring_gather(): second = lax.ppermute(down[half:], axis, shift(size, -1))]
    ppermute x12, starting transfers between devices: 14.4 us -> 12 us  [move(): return lax.ppermute(value, 'x', [(source, target)])]
    ppermute x3, starting transfers between devices: 12.2 us -> 14.5 us  [ring_gather(): down = lax.ppermute(down, axis, shift(size, -1))]
  transfers between devices with their start and end apart: 24 -> 24, of which waited for: 10 -> 8; matrix products, arithmetic and copies ran while one was open for 24% -> 25% of each run, Pallas kernels for 7% -> 4%
where the time goes in v3:
time: 217 us; the launch traced here: 216 us
  starting transfers between devices  63.1 us (29%)
  matrix products  38.5 us (18%)
  blocking collectives  38 us (18%)
  waiting for transfers between devices  37 us (17%)
  local copies, waits for them, and re-layouts  26.8 us (12%)
  Pallas kernels  9.8 us (5%)
    all_to_all x1, blocking collectives, send_sides(): came = lax.all_to_all(send, ROW, 0, 0, tiled=True)  19.2 us
    all_to_all x1, blocking collectives, on_device(): came = lax.all_to_all(send, ROW, 0, 0, tiled=True)  18.8 us
    ppermute x3, starting transfers between devices, ring_gather(): down = lax.ppermute(down, axis, shift(size, -1))  14.5 us
    all_to_all x1, starting transfers between devices, gather_blocks(): came = lax.all_to_all(send, ('x',) + Z, 0, 0, tiled=True)  13.7 us
    dot_general x20, matrix products, times(): lax.dot_general(jnp.concatenate([high, low], 0), right[0], dims, preferre...  12.4 us
    dynamic_update_slice x9, local copies, waits for them, and re-layouts, put(): lax.dynamic_update_slice(part, piece[None, i * rows:(i + 1) * rows], at)  12.1 us
    dot_general x20, matrix products, times(): lax.dot_general(high, right[1], dims, preferred_element_type=jnp.float32)  12.1 us
    ppermute x12, starting transfers between devices, move(): return lax.ppermute(value, 'x', [(source, target)])  12 us
  transfers between devices with their start and end apart: 24, of which 8 were waited for; matrix products, arithmetic and copies ran while one was open for 25% of the time, Pallas kernels for 4%

profile of v3, /device:TPU:1, one launch (start us, length us, event | category | flops | bytes accessed | tf_op | source)
XLA Modules:
  0.0 216.2 jit_solution(7445648766058134516)
XLA Ops:
  3.3 13.7 %all-to-all-start = ((f32[32,48,128]{2,1,0:T(8,128)}), f32[32,48,128]{2,1,0:T(8,128)S(1)}, u32[]{:S(2)}, u32[]{:S(2)}) async-start(f32[32,48,128]{2,1,0:T(8,128)} %bitcast.313), calls=%async_computation | async-start | bytes 1572864 | tf_op jit(solution)/shard_map/all_to_all | solution.py:147
  17.1 3.0 %add_convert_fusion.3 = bf16[64,8192]{1,0:T(8,128)(2,1)S(1)} fusion(f32[8,64]{1,0:T(8,128)S(1)} %bitcast.323, f32[8192]{0:T(1024)S(1)} %broadcast_multiply_fusion, f32[8,8192]{1,0:T(8,128)S(1)} %copy-done.6), kind=kOutput, calls=%fused_computation.19 | convolution fusion | flops 60358656 | bytes 1345536 | tf_op jit(solution)/shard_map/dot_general | solution.py:42
  20.1 3.0 %add_convert_fusion.2 = bf16[64,8192]{1,0:T(8,128)(2,1)S(1)} fusion(f32[8,64]{1,0:T(8,128)S(1)} %bitcast.322, f32[8192]{0:T(1024)S(1)} %broadcast_multiply_fusion, f32[8,8192]{1,0:T(8,128)S(1)} %copy-done.6), kind=kOutput, calls=%fused_computation.18 | convolution fusion | flops 60358656 | bytes 1345536 | tf_op jit(solution)/shard_map/dot_general | solution.py:42
  24.4 3.0 %add_convert_fusion.1 = bf16[64,8192]{1,0:T(8,128)(2,1)S(1)} fusion(f32[8,64]{1,0:T(8,128)S(1)} %bitcast.321, f32[8192]{0:T(1024)S(1)} %broadcast_multiply_fusion, f32[8,8192]{1,0:T(8,128)S(1)} %copy-done.6), kind=kOutput, calls=%fused_computation.17 | convolution fusion | flops 60358656 | bytes 1345536 | tf_op jit(solution)/shard_map/dot_general | solution.py:42
  28.0 3.0 %add_convert_fusion = bf16[64,8192]{1,0:T(8,128)(2,1)S(1)} fusion(f32[8,64]{1,0:T(8,128)S(1)} %bitcast.320, f32[8192]{0:T(1024)S(1)} %broadcast_multiply_fusion, f32[8,8192]{1,0:T(8,128)S(1)} %copy-done.6), kind=kOutput, calls=%fused_computation.16 | convolution fusion | flops 60358656 | bytes 1345536 | tf_op jit(solution)/shard_map/dot_general | solution.py:42
  33.8 2.5 %all-to-all-done.came_ref = f32[32,48,128]{2,1,0:T(8,128)S(1)} async-done(((f32[32,48,128]{2,1,0:T(8,128)}), f32[32,48,128]{2,1,0:T(8,128)S(1)}, u32[]{:S(2)}, u32[]{:S(2)}) %all-to-all-start) | async-done | bytes 786464 | tf_op jit(solution)/shard_map/all_to_all | solution.py:147
  39.1 5.1 %collective-permute-start = (f32[24,64,128]{2,1,0:T(8,128)S(1)}, f32[24,64,128]{2,1,0:T(8,128)}, u32[]{:S(2)}, u32[]{:S(2)}) collective-permute-start(f32[24,64,128]{2,1,0:T(8,128)S(1)} %spread_lanes.1), channel_id=1, source_target_pairs={{0,28},{4,0},{8,4},{12,8},{16,12},{20,16},{24,20},{28,24},{1,29},{... | collective-permute-start | bytes 2359304 | tf_op jit(solution)/shard_map/ppermute | solution.py:76
  46.1 19.2 %all_to_all.15 = f32[16,16,128]{2,1,0:T(8,128)} all-to-all(f32[16,16,128]{2,1,0:T(8,128)S(1)} %reshape.71), channel_id=1, replica_groups=mesh['x'=4,'zh'=2,'core'=2,'y'=8,'zl'=4] {'x','zh','core'}, dimensions={0} | all-to-all | bytes 262144 | tf_op jit(solution)/shard_map/all_to_all | solution.py:190
  68.5 4.9 %collective-permute-start.3 = (f32[24,64,128]{2,1,0:T(8,128)}, f32[24,64,128]{2,1,0:T(8,128)}, u32[]{:S(2)}, u32[]{:S(2)}) collective-permute-start(f32[24,64,128]{2,1,0:T(8,128)} %collective-permute-done), channel_id=1, source_target_pairs={{0,28},{4,0},{8,4},{12,8},{16,12},{20,16},{24,20},{28,24},{1,29},{... | collective-permute-start | bytes 2359304 | tf_op jit(solution)/shard_map/ppermute | solution.py:76
  80.5 8.4 %collective-permute-done.2 = f32[24,64,128]{2,1,0:T(8,128)} collective-permute-done((f32[24,64,128]{2,1,0:T(8,128)}, f32[24,64,128]{2,1,0:T(8,128)}, u32[]{:S(2)}, u32[]{:S(2)}) %collective-permute-start.2) | collective-permute-done | bytes 786464 | tf_op jit(solution)/shard_map/ppermute | solution.py:75
  90.8 4.6 %collective-permute-start.5 = (f32[24,64,128]{2,1,0:T(8,128)}, f32[24,64,128]{2,1,0:T(8,128)S(1)}, u32[]{:S(2)}, u32[]{:S(2)}) collective-permute-start(f32[24,64,128]{2,1,0:T(8,128)} %collective-permute-done.3), channel_id=1, source_target_pairs={{0,28},{4,0},{8,4},{12,8},{16,12},{20,16},{24,20},{28,24},{1,29},{... | collective-permute-start | bytes 2359304 | tf_op jit(solution)/shard_map/ppermute | solution.py:76
  101.5 2.1 fusion.19
  103.5 7.4 %collective-permute-done.5 = f32[24,64,128]{2,1,0:T(8,128)S(1)} collective-permute-done((f32[24,64,128]{2,1,0:T(8,128)}, f32[24,64,128]{2,1,0:T(8,128)S(1)}, u32[]{:S(2)}, u32[]{:S(2)}) %collective-permute-start.5) | collective-permute-done | bytes 786464 | tf_op jit(solution)/shard_map/ppermute | solution.py:76
  111.0 5.2 %collective-permute-start.7 = (f32[12,64,128]{2,1,0:T(8,128)S(1)}, f32[12,64,128]{2,1,0:T(8,128)S(1)}, u32[]{:S(2)}, u32[]{:S(2)}) collective-permute-start(f32[12,64,128]{2,1,0:T(8,128)S(1)} %slice.492), channel_id=1, source_target_pairs={{0,28},{4,0},{8,4},{12,8},{16,12},{20,16},{24,20},{28,24},{1,29},{... | collective-permute-start | bytes 1179656 | tf_op jit(solution)/shard_map/ppermute | solution.py:84
  120.1 2.0 collective-permute-done.7
  122.1 5.1 %collective-permute-done.6 = f32[12,64,128]{2,1,0:T(8,128)S(1)} collective-permute-done((f32[12,64,128]{2,1,0:T(8,128)S(1)}, f32[12,64,128]{2,1,0:T(8,128)S(1)}, u32[]{:S(2)}, u32[]{:S(2)}) %collective-permute-start.6) | collective-permute-done | bytes 393248 | tf_op jit(solution)/shard_map/ppermute | solution.py:83
  128.1 5.6 %collective-permute-start.9 = (f32[8,8,64,128]{3,2,1,0:T(8,128)}, f32[8,8,64,128]{3,2,1,0:T(8,128)}, u32[]{:S(2)}, u32[]{:S(2)}) collective-permute-start(f32[8,8,64,128]{3,2,1,0:T(8,128)} %get-tuple-element.63.own_ref), channel_id=1, source_target_pairs={{0,32},{32,0},{1,33},{33,1},{2,34},{34,2},{3,35},{35,3},{4,36},{36... | collective-permute-start | bytes 6291464 | tf_op jit(solution)/shard_map/ppermute | solution.py:159
  135.6 2.4 %collective-permute-start.11 = (f32[8,8,64,128]{3,2,1,0:T(8,128)}, f32[8,8,64,128]{3,2,1,0:T(8,128)}, u32[]{:S(2)}, u32[]{:S(2)}) collective-permute-start(f32[8,8,64,128]{3,2,1,0:T(8,128)} %get-tuple-element.61.own_ref), channel_id=1, source_target_pairs={{0,32},{32,0},{1,33},{33,1},{2,34},{34,2},{3,35},{35,3},{4,36},{36... | collective-permute-start | bytes 6291464 | tf_op jit(solution)/shard_map/ppermute | solution.py:159
  138.1 3.0 %lay_out.3 = (bf16[8,2,64,1024]{3,2,1,0:T(8,128)(2,1)S(1)}, bf16[8,2,64,1024]{3,2,1,0:T(8,128)(2,1)S(1)}) custom-call(s32[1]{0:T(128)} %bitcast.51.core_ref, f32[8,8,64,128]{3,2,1,0:T(8,128)} %get-tuple-element.63.own_ref, f32[8,8,64,128]{3,2,1,0:T(8,128)} %collective-permute-done.9.other_ref), custom_call_target="tpu_custom_call" | custom-call | tf_op jit(solution)/shard_map/lay_out/pallas_call | solution.py:164
  145.3 3.0 %lay_out.4 = (bf16[8,2,64,1024]{3,2,1,0:T(8,128)(2,1)S(1)}, bf16[8,2,64,1024]{3,2,1,0:T(8,128)(2,1)S(1)}) custom-call(s32[1]{0:T(128)} %bitcast.51.core_ref, f32[8,8,64,128]{3,2,1,0:T(8,128)} %get-tuple-element.62.own_ref, f32[8,8,64,128]{3,2,1,0:T(8,128)} %collective-permute-done.8.other_ref), custom_call_target="tpu_custom_call" | custom-call | tf_op jit(solution)/shard_map/lay_out/pallas_call | solution.py:164
  148.4 3.0 %lay_out.5 = (bf16[8,2,64,1024]{3,2,1,0:T(8,128)(2,1)S(1)}, bf16[8,2,64,1024]{3,2,1,0:T(8,128)(2,1)S(1)}) custom-call(s32[1]{0:T(128)} %bitcast.51.core_ref, f32[8,8,64,128]{3,2,1,0:T(8,128)} %get-tuple-element.61.own_ref, f32[8,8,64,128]{3,2,1,0:T(8,128)} %collective-permute-done.11.other_ref), custom_call_target="tpu_custom_call" | custom-call | tf_op jit(solution)/shard_map/lay_out/pallas_call | solution.py:164
  179.2 2.7 %collective-permute-done.19 = f32[32,1024]{1,0:T(8,128)S(1)} collective-permute-done((f32[32,1024]{1,0:T(8,128)S(1)}, f32[32,1024]{1,0:T(8,128)S(1)}, u32[]{:S(2)}, u32[]{:S(2)}) %collective-permute-start.19) | collective-permute-done | bytes 131104 | tf_op jit(solution)/shard_map/ppermute | solution.py:198
  187.8 7.0 %collective-permute-done.22 = f32[32,1024]{1,0:T(8,128)S(1)} collective-permute-done((f32[32,1024]{1,0:T(8,128)S(1)}, f32[32,1024]{1,0:T(8,128)S(1)}, u32[]{:S(2)}, u32[]{:S(2)}) %collective-permute-start.22) | collective-permute-done | bytes 131104 | tf_op jit(solution)/shard_map/ppermute | solution.py:198
  196.2 18.8 %all_to_all.16 = f32[16,16,128]{2,1,0:T(8,128)S(1)} all-to-all(f32[16,16,128]{2,1,0:T(8,128)S(1)} %reshape.80), channel_id=1, replica_groups=mesh['x'=4,'zh'=2,'core'=2,'y'=8,'zl'=4] {'x','zh','core'}, dimensions={0} | all-to-all | bytes 262144 | tf_op jit(solution)/shard_map/all_to_all | solution.py:228
  (143 shorter events, 77.4 us)
Async XLA Ops:
  3.3 33.0 %all-to-all-start = ((f32[32,48,128]{2,1,0:T(8,128)}), f32[32,48,128]{2,1,0:T(8,128)S(1)}, u32[]{:S(2)}, u32[]{:S(2)}) async-start(f32[32,48,128]{2,1,0:T(8,128)} %bitcast.313), calls=%async_computation | async-start | bytes 1572864 | tf_op jit(solution)/shard_map/all_to_all | solution.py:147
  39.1 27.5 %collective-permute-start = (f32[24,64,128]{2,1,0:T(8,128)S(1)}, f32[24,64,128]{2,1,0:T(8,128)}, u32[]{:S(2)}, u32[]{:S(2)}) collective-permute-start(f32[24,64,128]{2,1,0:T(8,128)S(1)} %spread_lanes.1), channel_id=1, source_target_pairs={{0,28},{4,0},{8,4},{12,8},{16,12},{20,16},{24,20},{28,24},{1,29},{... | collective-permute-start | bytes 2359304 | tf_op jit(solution)/shard_map/ppermute | solution.py:76
  44.2 22.4 %collective-permute-start.1 = (f32[24,64,128]{2,1,0:T(8,128)S(1)}, f32[24,64,128]{2,1,0:T(8,128)}, u32[]{:S(2)}, u32[]{:S(2)}) collective-permute-start(f32[24,64,128]{2,1,0:T(8,128)S(1)} %spread_lanes.1), channel_id=1, source_target_pairs={{0,4},{4,8},{8,12},{12,16},{16,20},{20,24},{24,28},{28,0},{1,5},{5... | collective-permute-start | bytes 2359304 | tf_op jit(solution)/shard_map/ppermute | solution.py:75
  66.6 22.3 %collective-permute-start.2 = (f32[24,64,128]{2,1,0:T(8,128)}, f32[24,64,128]{2,1,0:T(8,128)}, u32[]{:S(2)}, u32[]{:S(2)}) collective-permute-start(f32[24,64,128]{2,1,0:T(8,128)} %collective-permute-done.1), channel_id=1, source_target_pairs={{0,4},{4,8},{8,12},{12,16},{16,20},{20,24},{24,28},{28,0},{1,5},{5... | collective-permute-start | bytes 2359304 | tf_op jit(solution)/shard_map/ppermute | solution.py:75
  68.5 22.3 %collective-permute-start.3 = (f32[24,64,128]{2,1,0:T(8,128)}, f32[24,64,128]{2,1,0:T(8,128)}, u32[]{:S(2)}, u32[]{:S(2)}) collective-permute-start(f32[24,64,128]{2,1,0:T(8,128)} %collective-permute-done), channel_id=1, source_target_pairs={{0,28},{4,0},{8,4},{12,8},{16,12},{20,16},{24,20},{28,24},{1,29},{... | collective-permute-start | bytes 2359304 | tf_op jit(solution)/shard_map/ppermute | solution.py:76
  88.9 27.3 %collective-permute-start.4 = (f32[24,64,128]{2,1,0:T(8,128)}, f32[24,64,128]{2,1,0:T(8,128)S(1)}, u32[]{:S(2)}, u32[]{:S(2)}) collective-permute-start(f32[24,64,128]{2,1,0:T(8,128)} %collective-permute-done.2), channel_id=1, source_target_pairs={{0,4},{4,8},{8,12},{12,16},{16,20},{20,24},{24,28},{28,0},{1,5},{5... | collective-permute-start | bytes 2359304 | tf_op jit(solution)/shard_map/ppermute | solution.py:75
  90.8 20.1 %collective-permute-start.5 = (f32[24,64,128]{2,1,0:T(8,128)}, f32[24,64,128]{2,1,0:T(8,128)S(1)}, u32[]{:S(2)}, u32[]{:S(2)}) collective-permute-start(f32[24,64,128]{2,1,0:T(8,128)} %collective-permute-done.3), channel_id=1, source_target_pairs={{0,28},{4,0},{8,4},{12,8},{16,12},{20,16},{24,20},{28,24},{1,29},{... | collective-permute-start | bytes 2359304 | tf_op jit(solution)/shard_map/ppermute | solution.py:76
  111.0 11.1 %collective-permute-start.7 = (f32[12,64,128]{2,1,0:T(8,128)S(1)}, f32[12,64,128]{2,1,0:T(8,128)S(1)}, u32[]{:S(2)}, u32[]{:S(2)}) collective-permute-start(f32[12,64,128]{2,1,0:T(8,128)S(1)} %slice.492), channel_id=1, source_target_pairs={{0,28},{4,0},{8,4},{12,8},{16,12},{20,16},{24,20},{28,24},{1,29},{... | collective-permute-start | bytes 1179656 | tf_op jit(solution)/shard_map/ppermute | solution.py:84
  116.3 10.9 %collective-permute-start.6 = (f32[12,64,128]{2,1,0:T(8,128)S(1)}, f32[12,64,128]{2,1,0:T(8,128)S(1)}, u32[]{:S(2)}, u32[]{:S(2)}) collective-permute-start(f32[12,64,128]{2,1,0:T(8,128)S(1)} %slice.491), channel_id=1, source_target_pairs={{0,4},{4,8},{8,12},{12,16},{16,20},{20,24},{24,28},{28,0},{1,5},{5... | collective-permute-start | bytes 1179656 | tf_op jit(solution)/shard_map/ppermute | solution.py:83
  128.1 10.0 %collective-permute-start.9 = (f32[8,8,64,128]{3,2,1,0:T(8,128)}, f32[8,8,64,128]{3,2,1,0:T(8,128)}, u32[]{:S(2)}, u32[]{:S(2)}) collective-permute-start(f32[8,8,64,128]{3,2,1,0:T(8,128)} %get-tuple-element.63.own_ref), channel_id=1, source_target_pairs={{0,32},{32,0},{1,33},{33,1},{2,34},{34,2},{3,35},{35,3},{4,36},{36... | collective-permute-start | bytes 6291464 | tf_op jit(solution)/shard_map/ppermute | solution.py:159
  133.7 7.4 %collective-permute-start.8 = (f32[8,8,64,128]{3,2,1,0:T(8,128)}, f32[8,8,64,128]{3,2,1,0:T(8,128)}, u32[]{:S(2)}, u32[]{:S(2)}) collective-permute-start(f32[8,8,64,128]{3,2,1,0:T(8,128)} %get-tuple-element.62.own_ref), channel_id=1, source_target_pairs={{0,32},{32,0},{1,33},{33,1},{2,34},{34,2},{3,35},{35,3},{4,36},{36... | collective-permute-start | bytes 6291464 | tf_op jit(solution)/shard_map/ppermute | solution.py:159
  135.6 12.7 %collective-permute-start.11 = (f32[8,8,64,128]{3,2,1,0:T(8,128)}, f32[8,8,64,128]{3,2,1,0:T(8,128)}, u32[]{:S(2)}, u32[]{:S(2)}) collective-permute-start(f32[8,8,64,128]{3,2,1,0:T(8,128)} %get-tuple-element.61.own_ref), channel_id=1, source_target_pairs={{0,32},{32,0},{1,33},{33,1},{2,34},{34,2},{3,35},{35,3},{4,36},{36... | collective-permute-start | bytes 6291464 | tf_op jit(solution)/shard_map/ppermute | solution.py:159
  142.7 15.9 %collective-permute-start.12 = (f32[32,1024]{1,0:T(8,128)S(1)}, f32[32,1024]{1,0:T(8,128)S(1)}, u32[]{:S(2)}, u32[]{:S(2)}) collective-permute-start(f32[32,1024]{1,0:T(8,128)S(1)} %get-tuple-element.120), channel_id=1, source_target_pairs={{0,256},{1,257},{2,258},{3,259},{4,260},{5,261},{6,262},{7,263},{8... | collective-permute-start | bytes 393224 | tf_op jit(solution)/shard_map/ppermute | solution.py:198
  144.0 10.2 %collective-permute-start.10 = (f32[32,1024]{1,0:T(8,128)S(1)}, f32[32,1024]{1,0:T(8,128)S(1)}, u32[]{:S(2)}, u32[]{:S(2)}) collective-permute-start(f32[32,1024]{1,0:T(8,128)S(1)} %get-tuple-element.120), channel_id=1, source_target_pairs={{0,128},{1,129},{2,130},{3,131},{4,132},{5,133},{6,134},{7,135},{8... | collective-permute-start | bytes 393224 | tf_op jit(solution)/shard_map/ppermute | solution.py:198
  152.9 13.5 %collective-permute-start.14 = (f32[32,1024]{1,0:T(8,128)S(1)}, f32[32,1024]{1,0:T(8,128)S(1)}, u32[]{:S(2)}, u32[]{:S(2)}) collective-permute-start(f32[32,1024]{1,0:T(8,128)S(1)} %convolution_add_fusion.17), channel_id=1, source_target_pairs={{0,384},{1,385},{2,386},{3,387},{4,388},{5,389},{6,390},{7,391},{8... | collective-permute-start | bytes 393224 | tf_op jit(solution)/shard_map/ppermute | solution.py:198
  157.3 2.2 collective-permute-start.13
  157.9 6.1 %collective-permute-start.15 = (f32[32,1024]{1,0:T(8,128)S(1)}, f32[32,1024]{1,0:T(8,128)S(1)}, u32[]{:S(2)}, u32[]{:S(2)}) collective-permute-start(f32[32,1024]{1,0:T(8,128)S(1)} %convolution_add_fusion.21), channel_id=1, source_target_pairs={{128,384},{129,385},{130,386},{131,387},{132,388},{133,389},{134,3... | collective-permute-start | bytes 393224 | tf_op jit(solution)/shard_map/ppermute | solution.py:198
  163.2 2.4 %collective-permute-start.16 = (f32[32,1024]{1,0:T(8,128)S(1)}, f32[32,1024]{1,0:T(8,128)S(1)}, u32[]{:S(2)}, u32[]{:S(2)}) collective-permute-start(f32[32,1024]{1,0:T(8,128)S(1)} %convolution_add_fusion.18), channel_id=1, source_target_pairs={{256,384},{257,385},{258,386},{259,387},{260,388},{261,389},{262,3... | collective-permute-start | bytes 393224 | tf_op jit(solution)/shard_map/ppermute | solution.py:198
  171.1 3.1 %collective-permute-start.17 = (f32[32,1024]{1,0:T(8,128)S(1)}, f32[32,1024]{1,0:T(8,128)S(1)}, u32[]{:S(2)}, u32[]{:S(2)}) collective-permute-start(f32[32,1024]{1,0:T(8,128)S(1)} %convolution_add_fusion.12), channel_id=1, source_target_pairs={{384,256},{385,257},{386,258},{387,259},{388,260},{389,261},{390,2... | collective-permute-start | bytes 393224 | tf_op jit(solution)/shard_map/ppermute | solution.py:198
  171.8 10.0 %collective-permute-start.19 = (f32[32,1024]{1,0:T(8,128)S(1)}, f32[32,1024]{1,0:T(8,128)S(1)}, u32[]{:S(2)}, u32[]{:S(2)}) collective-permute-start(f32[32,1024]{1,0:T(8,128)S(1)} %get-tuple-element.122), channel_id=1, source_target_pairs={{384,0},{385,1},{386,2},{387,3},{388,4},{389,5},{390,6},{391,7},{3... | collective-permute-start | bytes 393224 | tf_op jit(solution)/shard_map/ppermute | solution.py:198
  173.5 8.8 %collective-permute-start.20 = (f32[32,1024]{1,0:T(8,128)S(1)}, f32[32,1024]{1,0:T(8,128)S(1)}, u32[]{:S(2)}, u32[]{:S(2)}) collective-permute-start(f32[32,1024]{1,0:T(8,128)S(1)} %convolution_add_fusion.8), channel_id=1, source_target_pairs={{384,128},{385,129},{386,130},{387,131},{388,132},{389,133},{390,1... | collective-permute-start | bytes 393224 | tf_op jit(solution)/shard_map/ppermute | solution.py:198
  176.7 11.1 %collective-permute-start.18 = (f32[32,1024]{1,0:T(8,128)S(1)}, f32[32,1024]{1,0:T(8,128)S(1)}, u32[]{:S(2)}, u32[]{:S(2)}) collective-permute-start(f32[32,1024]{1,0:T(8,128)S(1)} %convolution_add_fusion.10), channel_id=1, source_target_pairs={{256,0},{257,1},{258,2},{259,3},{260,4},{261,5},{262,6},{263,7},{2... | collective-permute-start | bytes 393224 | tf_op jit(solution)/shard_map/ppermute | solution.py:198
  178.5 3.9 %collective-permute-start.21 = (f32[32,1024]{1,0:T(8,128)S(1)}, f32[32,1024]{1,0:T(8,128)S(1)}, u32[]{:S(2)}, u32[]{:S(2)}) collective-permute-start(f32[32,1024]{1,0:T(8,128)S(1)} %convolution_add_fusion.7), channel_id=1, source_target_pairs={{256,128},{257,129},{258,130},{259,131},{260,132},{261,133},{262,1... | collective-permute-start | bytes 393224 | tf_op jit(solution)/shard_map/ppermute | solution.py:198
  184.3 10.5 %collective-permute-start.22 = (f32[32,1024]{1,0:T(8,128)S(1)}, f32[32,1024]{1,0:T(8,128)S(1)}, u32[]{:S(2)}, u32[]{:S(2)}) collective-permute-start(f32[32,1024]{1,0:T(8,128)S(1)} %convolution_add_fusion.5), channel_id=1, source_target_pairs={{128,0},{129,1},{130,2},{131,3},{132,4},{133,5},{134,6},{135,7},{1... | collective-permute-start | bytes 393224 | tf_op jit(solution)/shard_map/ppermute | solution.py:198
  (7 other events, 79.5 us)

commit v4 on v3

--- a/solution.py
+++ b/solution.py
@@ -17,11 +17,12 @@
 Z = ("zh", "zl")
 
 HELD = (
-    ((0, 0), None, (3, 0)),
-    ((1, 1), (1, 0), None),
+    ((0, 0), (3, 0), (2, 0)),
+    ((1, 1), (1, 0), (3, 1)),
     ((2, 2), (2, 1), (2, 0)),
     ((3, 3), (3, 2), (3, 1)),
 )
+PARTS = ((0, 8), (8, 16), (16, 20))
 
 
 def cos_coefficients():
@@ -59,13 +60,12 @@
 
 def ring_gather(unit, axis, size, parts, beside):
     here = lax.axis_index(axis)
-    rows = unit.shape[0] // parts
-    held = [jnp.zeros((size, rows) + unit.shape[1:], unit.dtype) for _ in range(parts)]
+    held = [jnp.zeros((size, end - start) + unit.shape[1:], unit.dtype) for start, end in parts]
 
     def put(held, piece, step):
         at = (lax.rem(here + step + size, size),) + (0,) * unit.ndim
         return [
-            lax.dynamic_update_slice(part, piece[None, i * rows : (i + 1) * rows], at) for i, part in enumerate(held)
+            lax.dynamic_update_slice(part, piece[None, start:end], at) for part, (start, end) in zip(held, parts)
         ]
 
     held = put(held, unit, 0)
@@ -151,16 +151,18 @@
         compiler_params=pltpu.CompilerParams(vmem_limit_bytes=16 * 1024 * 1024),
         name="spread_lanes",
     )(came)
+    upper = lax.axis_index("x") >= 2
+    unit = jnp.concatenate([unit[:16], jnp.where(upper, unit[16:20], unit[20:])], 0)
     unit, sides = lax.optimization_barrier((unit, sides))
-    held, right = ring_gather(unit, "y", 8, 3, lambda: send_sides(sides))
+    held, right = ring_gather(unit, "y", 8, PARTS, lambda: send_sides(sides))
     core = lax.axis_index("core").reshape(1).astype(jnp.int32)
     whole = pl.BlockSpec(memory_space=pltpu.VMEM)
-    shape = jax.ShapeDtypeStruct((8, 2, share, 32 * k), jnp.bfloat16)
     others = [lax.ppermute(part, "core", shift(2, 1)) for part in held]
     found = []
     for own, other in zip(held, others):
         if found:
             other, found[-1] = lax.optimization_barrier((other, found[-1]))
+        shape = jax.ShapeDtypeStruct((own.shape[1], 2, share, 32 * k), jnp.bfloat16)
         both = pl.pallas_call(
             lay_out,
             in_specs=[pl.BlockSpec(memory_space=pltpu.SMEM), whole, whole],
@@ -169,7 +171,7 @@
             compiler_params=pltpu.CompilerParams(vmem_limit_bytes=16 * 1024 * 1024),
             name="lay_out",
         )(core, own, other)
-        found.append(tuple(half.reshape(16 * share, 32 * k) for half in both))
+        found.append(tuple(half.reshape(-1, 32 * k) for half in both))
     return found, right
 
 
@@ -197,30 +199,42 @@
     def move(value, source, target):
         return lax.ppermute(value, "x", [(source, target)])
 
+    def beyond(value):
+        return jnp.concatenate([value, times(value, third, 1)], 1)
+
+    def whole_third(skip):
+        return jnp.concatenate([times(skip[:, :size], third, 1), skip[:, size:]], 1)
+
+    def beyond_back(value):
+        return jnp.concatenate([times(value[:, : size // 2], third, 0), value[:, size // 2 :]], 1)
+
+    def whole_third_back(skip):
+        return skip[:, :size] + times(skip[:, size:], third, 0)
+
     first = times(right, diagonal, 1)
     near = move(first, 0, 1)
-    skip = move(first, 0, 2)
-    far = move(times(first, third, 1), 0, 3)
+    skip = move(beyond(first), 0, 2)
+    far = move(times(first, beside, 1), 0, 3)
     second = times(right - times(near, beside, 1), diagonal, 1)
     near = move(second, 1, 2)
-    skip_on = move(second, 1, 3)
-    base = right - times(skip, third, 1)
+    skip_on = move(beyond(second), 1, 3)
+    base = right - whole_third(skip)
     solved = times(base - times(near, beside, 1), diagonal, 1)
     near = move(solved, 2, 3)
-    base = right - far - times(skip_on, third, 1)
+    base = right - far - whole_third(skip_on)
     last = times(base - times(near, beside, 1), diagonal, 1)
     mine = jnp.where(here == 0, first, jnp.where(here == 1, second, jnp.where(here == 2, solved, last)))
 
     fourth = times(mine, diagonal, 0)
     near = move(times(fourth, beside, 0), 3, 2)
     far = move(fourth, 3, 0)
-    skip = move(times(fourth, third, 0), 3, 1)
+    skip = move(beyond_back(fourth), 3, 1)
     answer = times(mine - near, diagonal, 0)
     near = move(times(answer, beside, 0), 2, 1)
-    skip_on = move(times(answer, third, 0), 2, 0)
-    second = times(mine - skip - near, diagonal, 0)
+    skip_on = move(beyond_back(answer), 2, 0)
+    second = times(mine - whole_third_back(skip) - near, diagonal, 0)
     near = move(times(second, beside, 0), 1, 0)
-    base = mine - skip_on - times(far, third, 0)
+    base = mine - whole_third_back(skip_on) - times(far, beside, 0)
     first = times(base - near, diagonal, 0)
     result = jnp.where(here == 0, first, jnp.where(here == 1, second, jnp.where(here == 2, answer, fourth)))
 

time: 217 us -> 211 us (0.972)
  blocking collectives: 38 us -> 19.5 us
  starting transfers between devices: 63.1 us -> 72.8 us
    all_to_all x1 -> x0, blocking collectives: 19.2 us -> none  [send_sides(): came = lax.all_to_all(send, ROW, 0, 0, tiled=True)]
    ppermute x3, waiting for transfers between devices: 8.45 us -> 20.3 us  [ring_gather(): up = lax.ppermute(up, axis, shift(size, 1))]
    all_to_all x0 -> x1, starting transfers between devices: none -> 9.18 us  [send_sides(): came = lax.all_to_all(send, ROW, 0, 0, tiled=True)]
    ppermute x3, waiting for transfers between devices: 7.45 us -> 0.01 us  [ring_gather(): down = lax.ppermute(down, axis, shift(size, -1))]
    ppermute x1, waiting for transfers between devices: 5.09 us -> 1.28 us  [ring_gather(): first = lax.ppermute(up[:half], axis, shift(size, 1))]
    all_to_all x0 -> x1, waiting for transfers between devices: none -> 2.52 us  [send_sides(): came = lax.all_to_all(send, ROW, 0, 0, tiled=True)]
    ppermute x3, starting transfers between devices: 14.5 us -> 12 us  [ring_gather(): down = lax.ppermute(down, axis, shift(size, -1))]
    another operation x5 -> x2, local copies, waits for them, and re-layouts: 4.9 us -> 3.26 us
  transfers between devices with their start and end apart: 24 -> 25, of which waited for: 8 -> 9; matrix products, arithmetic and copies ran while one was open for 25% -> 27% of each run, Pallas kernels for 4% -> 3%
where the time goes in v4:
time: 211 us; the launch traced here: 209 us
  starting transfers between devices  72.8 us (35%)
  matrix products  39.5 us (19%)
  waiting for transfers between devices  38.7 us (18%)
  local copies, waits for them, and re-layouts  25.9 us (12%)
  blocking collectives  19.5 us (9%)
  Pallas kernels  8.39 us (4%)
  other arithmetic  3.3 us (2%)
    ppermute x3, waiting for transfers between devices, ring_gather(): up = lax.ppermute(up, axis, shift(size, 1))  20.3 us
    all_to_all x1, blocking collectives, on_device(): came = lax.all_to_all(send, ROW, 0, 0, tiled=True)  19.5 us
    ppermute x12, starting transfers between devices, move(): return lax.ppermute(value, 'x', [(source, target)])  14.2 us
    all_to_all x1, starting transfers between devices, gather_blocks(): came = lax.all_to_all(send, ('x',) + Z, 0, 0, tiled=True)  13.7 us
    dynamic_update_slice x16, local copies, waits for them, and re-layouts, put(): lax.dynamic_update_slice(part, piece[None, start:end], at)  13.4 us
    dot_general x24, matrix products, times(): lax.dot_general(jnp.concatenate([high, low], 0), right[0], dims, preferre...  12.9 us
    dot_general x24, matrix products, times(): lax.dot_general(high, right[1], dims, preferred_element_type=jnp.float32)  12.6 us
    ppermute x3, starting transfers between devices, ring_gather(): down = lax.ppermute(down, axis, shift(size, -1))  12 us
  transfers between devices with their start and end apart: 25, of which 9 were waited for; matrix products, arithmetic and copies ran while one was open for 27% of the time, Pallas kernels for 3%

profile of v4, /device:TPU:1, one launch (start us, length us, event | category | flops | bytes accessed | tf_op | source)
XLA Modules:
  0.0 209.1 jit_solution(12707058429054895141)
XLA Ops:
  3.3 13.7 %all-to-all-start = ((f32[32,48,128]{2,1,0:T(8,128)}), f32[32,48,128]{2,1,0:T(8,128)S(1)}, u32[]{:S(2)}, u32[]{:S(2)}) async-start(f32[32,48,128]{2,1,0:T(8,128)} %bitcast.333), calls=%async_computation | async-start | bytes 1572864 | tf_op jit(solution)/shard_map/all_to_all | solution.py:147
  17.1 3.0 %add_convert_fusion.2 = bf16[64,8192]{1,0:T(8,128)(2,1)S(1)} fusion(f32[8,64]{1,0:T(8,128)S(1)} %bitcast.343, f32[8192]{0:T(1024)S(1)} %broadcast_multiply_fusion, f32[8,8192]{1,0:T(8,128)S(1)} %copy-done.4), kind=kOutput, calls=%fused_computation.18 | convolution fusion | flops 60358656 | bytes 1345536 | tf_op jit(solution)/shard_map/dot_general | solution.py:43
  20.1 3.0 %add_convert_fusion.1 = bf16[64,8192]{1,0:T(8,128)(2,1)S(1)} fusion(f32[8,64]{1,0:T(8,128)S(1)} %bitcast.342, f32[8192]{0:T(1024)S(1)} %broadcast_multiply_fusion, f32[8,8192]{1,0:T(8,128)S(1)} %copy-done.4), kind=kOutput, calls=%fused_computation.17 | convolution fusion | flops 60358656 | bytes 1345536 | tf_op jit(solution)/shard_map/dot_general | solution.py:43
  24.3 3.0 %add_convert_fusion = bf16[64,8192]{1,0:T(8,128)(2,1)S(1)} fusion(f32[8,64]{1,0:T(8,128)S(1)} %bitcast.341, f32[8192]{0:T(1024)S(1)} %broadcast_multiply_fusion, f32[8,8192]{1,0:T(8,128)S(1)} %copy-done.4), kind=kOutput, calls=%fused_computation.16 | convolution fusion | flops 60358656 | bytes 1345536 | tf_op jit(solution)/shard_map/dot_general | solution.py:43
  27.9 3.0 %add_convert_fusion.3 = bf16[64,8192]{1,0:T(8,128)(2,1)S(1)} fusion(f32[8,64]{1,0:T(8,128)S(1)} %bitcast.340, f32[8192]{0:T(1024)S(1)} %broadcast_multiply_fusion, f32[8,8192]{1,0:T(8,128)S(1)} %copy-done.4), kind=kOutput, calls=%fused_computation.19 | convolution fusion | flops 60358656 | bytes 1345536 | tf_op jit(solution)/shard_map/dot_general | solution.py:43
  37.9 3.2 %collective-permute-start.1 = (f32[20,64,128]{2,1,0:T(8,128)}, f32[20,64,128]{2,1,0:T(8,128)}, u32[]{:S(2)}, u32[]{:S(2)}) collective-permute-start(f32[20,64,128]{2,1,0:T(8,128)} %pad_maximum_fusion), channel_id=1, source_target_pairs={{0,4},{4,8},{8,12},{12,16},{16,20},{20,24},{24,28},{28,0},{1,5},{5... | collective-permute-start | bytes 1966088 | tf_op jit(solution)/shard_map/ppermute | solution.py:75
  41.1 3.8 %collective-permute-start = (f32[20,64,128]{2,1,0:T(8,128)}, f32[20,64,128]{2,1,0:T(8,128)}, u32[]{:S(2)}, u32[]{:S(2)}) collective-permute-start(f32[20,64,128]{2,1,0:T(8,128)} %pad_maximum_fusion), channel_id=1, source_target_pairs={{0,28},{4,0},{8,4},{12,8},{16,12},{20,16},{24,20},{28,24},{1,29},{... | collective-permute-start | bytes 1966088 | tf_op jit(solution)/shard_map/ppermute | solution.py:76
  44.9 9.2 %all-to-all-start.1 = ((f32[16,16,128]{2,1,0:T(8,128)}), f32[16,16,128]{2,1,0:T(8,128)S(1)}, u32[]{:S(2)}, u32[]{:S(2)}) async-start(f32[16,16,128]{2,1,0:T(8,128)} %reshape.71), calls=%async_computation.1 | async-start | bytes 262144 | tf_op jit(solution)/shard_map/all_to_all | solution.py:192
  61.7 2.5 %all-to-all-done.1 = f32[16,16,128]{2,1,0:T(8,128)S(1)} async-done(((f32[16,16,128]{2,1,0:T(8,128)}), f32[16,16,128]{2,1,0:T(8,128)S(1)}, u32[]{:S(2)}, u32[]{:S(2)}) %all-to-all-start.1) | async-done | bytes 131104 | tf_op jit(solution)/shard_map/all_to_all | solution.py:192
  66.5 3.6 %collective-permute-start.3 = (f32[20,64,128]{2,1,0:T(8,128)}, f32[20,64,128]{2,1,0:T(8,128)S(1)}, u32[]{:S(2)}, u32[]{:S(2)}) collective-permute-start(f32[20,64,128]{2,1,0:T(8,128)} %collective-permute-done), channel_id=1, source_target_pairs={{0,28},{4,0},{8,4},{12,8},{16,12},{20,16},{24,20},{28,24},{1,29},{... | collective-permute-start | bytes 1966088 | tf_op jit(solution)/shard_map/ppermute | solution.py:76
  76.8 12.0 %collective-permute-done.2 = f32[20,64,128]{2,1,0:T(8,128)S(1)} collective-permute-done((f32[20,64,128]{2,1,0:T(8,128)}, f32[20,64,128]{2,1,0:T(8,128)S(1)}, u32[]{:S(2)}, u32[]{:S(2)}) %collective-permute-start.2) | collective-permute-done | bytes 655392 | tf_op jit(solution)/shard_map/ppermute | solution.py:75
  90.7 4.6 %collective-permute-start.5 = (f32[20,64,128]{2,1,0:T(8,128)S(1)}, f32[20,64,128]{2,1,0:T(8,128)S(1)}, u32[]{:S(2)}, u32[]{:S(2)}) collective-permute-start(f32[20,64,128]{2,1,0:T(8,128)S(1)} %collective-permute-done.3), channel_id=1, source_target_pairs={{0,28},{4,0},{8,4},{12,8},{16,12},{20,16},{24,20},{28,24},{1,29},{... | collective-permute-start | bytes 1966088 | tf_op jit(solution)/shard_map/ppermute | solution.py:76
  97.9 8.3 %collective-permute-done.4 = f32[20,64,128]{2,1,0:T(8,128)S(1)} collective-permute-done((f32[20,64,128]{2,1,0:T(8,128)S(1)}, f32[20,64,128]{2,1,0:T(8,128)S(1)}, u32[]{:S(2)}, u32[]{:S(2)}) %collective-permute-start.4) | collective-permute-done | bytes 655392 | tf_op jit(solution)/shard_map/ppermute | solution.py:75
  106.2 1.9 collective-permute-start.6
  108.2 4.6 %collective-permute-start.7 = (f32[10,64,128]{2,1,0:T(8,128)S(1)}, f32[10,64,128]{2,1,0:T(8,128)S(1)}, u32[]{:S(2)}, u32[]{:S(2)}) collective-permute-start(f32[10,64,128]{2,1,0:T(8,128)S(1)} %slice.593), channel_id=1, source_target_pairs={{0,28},{4,0},{8,4},{12,8},{16,12},{20,16},{24,20},{28,24},{1,29},{... | collective-permute-start | bytes 983048 | tf_op jit(solution)/shard_map/ppermute | solution.py:84
  117.6 5.8 %collective-permute-start.9 = (f32[8,8,64,128]{3,2,1,0:T(8,128)}, f32[8,8,64,128]{3,2,1,0:T(8,128)}, u32[]{:S(2)}, u32[]{:S(2)}) collective-permute-start(f32[8,8,64,128]{3,2,1,0:T(8,128)} %get-tuple-element.57.own_ref), channel_id=1, source_target_pairs={{0,32},{32,0},{1,33},{33,1},{2,34},{34,2},{3,35},{35,3},{4,36},{36... | collective-permute-start | bytes 6291464 | tf_op jit(solution)/shard_map/ppermute | solution.py:160
  123.5 1.9 collective-permute-start.8
  125.5 2.4 %collective-permute-start.11 = (f32[8,4,64,128]{3,2,1,0:T(8,128)S(1)}, f32[8,4,64,128]{3,2,1,0:T(8,128)}, u32[]{:S(2)}, u32[]{:S(2)}) collective-permute-start(f32[8,4,64,128]{3,2,1,0:T(8,128)S(1)} %fusion.55.own_ref), channel_id=1, source_target_pairs={{0,32},{32,0},{1,33},{33,1},{2,34},{34,2},{3,35},{35,3},{4,36},{36... | collective-permute-start | bytes 3145736 | tf_op jit(solution)/shard_map/ppermute | solution.py:160
  128.0 3.0 %lay_out.3 = (bf16[8,2,64,1024]{3,2,1,0:T(8,128)(2,1)S(1)}, bf16[8,2,64,1024]{3,2,1,0:T(8,128)(2,1)S(1)}) custom-call(s32[1]{0:T(128)} %bitcast.51.core_ref, f32[8,8,64,128]{3,2,1,0:T(8,128)} %get-tuple-element.57.own_ref, f32[8,8,64,128]{3,2,1,0:T(8,128)} %collective-permute-done.9.other_ref), custom_call_target="tpu_custom_call" | custom-call | tf_op jit(solution)/shard_map/lay_out/pallas_call | solution.py:166
  131.0 3.0 %lay_out.4 = (bf16[8,2,64,1024]{3,2,1,0:T(8,128)(2,1)S(1)}, bf16[8,2,64,1024]{3,2,1,0:T(8,128)(2,1)S(1)}) custom-call(s32[1]{0:T(128)} %bitcast.51.core_ref, f32[8,8,64,128]{3,2,1,0:T(8,128)} %get-tuple-element.58.own_ref, f32[8,8,64,128]{3,2,1,0:T(8,128)} %collective-permute-done.8.other_ref), custom_call_target="tpu_custom_call" | custom-call | tf_op jit(solution)/shard_map/lay_out/pallas_call | solution.py:166
  137.2 3.5 %collective-permute-start.10 = (f32[32,1024]{1,0:T(8,128)S(1)}, f32[32,1024]{1,0:T(8,128)S(1)}, u32[]{:S(2)}, u32[]{:S(2)}) collective-permute-start(f32[32,1024]{1,0:T(8,128)S(1)} %get-tuple-element.127), channel_id=1, source_target_pairs={{0,128},{1,129},{2,130},{3,131},{4,132},{5,133},{6,134},{7,135},{8... | collective-permute-start | bytes 393224 | tf_op jit(solution)/shard_map/ppermute | solution.py:200
  175.6 6.8 %collective-permute-done.18 = f32[32,1536]{1,0:T(8,128)S(1)} collective-permute-done((f32[32,1536]{1,0:T(8,128)S(1)}, f32[32,1536]{1,0:T(8,128)S(1)}, u32[]{:S(2)}, u32[]{:S(2)}) %collective-permute-start.18) | collective-permute-done | bytes 196640 | tf_op jit(solution)/shard_map/ppermute | solution.py:200
  183.0 4.0 %collective-permute-done.22 = f32[32,1024]{1,0:T(8,128)S(1)} collective-permute-done((f32[32,1024]{1,0:T(8,128)S(1)}, f32[32,1024]{1,0:T(8,128)S(1)}, u32[]{:S(2)}, u32[]{:S(2)}) %collective-permute-start.22) | collective-permute-done | bytes 131104 | tf_op jit(solution)/shard_map/ppermute | solution.py:200
  188.4 19.5 %all_to_all.15 = f32[16,16,128]{2,1,0:T(8,128)S(1)} all-to-all(f32[16,16,128]{2,1,0:T(8,128)S(1)} %reshape.80), channel_id=1, replica_groups=mesh['x'=4,'zh'=2,'core'=2,'y'=8,'zl'=4] {'x','zh','core'}, dimensions={0} | all-to-all | bytes 262144 | tf_op jit(solution)/shard_map/all_to_all | solution.py:242
  (167 shorter events, 78.7 us)
Async XLA Ops:
  3.3 33.0 %all-to-all-start = ((f32[32,48,128]{2,1,0:T(8,128)}), f32[32,48,128]{2,1,0:T(8,128)S(1)}, u32[]{:S(2)}, u32[]{:S(2)}) async-start(f32[32,48,128]{2,1,0:T(8,128)} %bitcast.333), calls=%async_computation | async-start | bytes 1572864 | tf_op jit(solution)/shard_map/all_to_all | solution.py:147
  37.9 32.2 %collective-permute-start.1 = (f32[20,64,128]{2,1,0:T(8,128)}, f32[20,64,128]{2,1,0:T(8,128)}, u32[]{:S(2)}, u32[]{:S(2)}) collective-permute-start(f32[20,64,128]{2,1,0:T(8,128)} %pad_maximum_fusion), channel_id=1, source_target_pairs={{0,4},{4,8},{8,12},{12,16},{16,20},{20,24},{24,28},{28,0},{1,5},{5... | collective-permute-start | bytes 1966088 | tf_op jit(solution)/shard_map/ppermute | solution.py:75
  41.1 25.3 %collective-permute-start = (f32[20,64,128]{2,1,0:T(8,128)}, f32[20,64,128]{2,1,0:T(8,128)}, u32[]{:S(2)}, u32[]{:S(2)}) collective-permute-start(f32[20,64,128]{2,1,0:T(8,128)} %pad_maximum_fusion), channel_id=1, source_target_pairs={{0,28},{4,0},{8,4},{12,8},{16,12},{20,16},{24,20},{28,24},{1,29},{... | collective-permute-start | bytes 1966088 | tf_op jit(solution)/shard_map/ppermute | solution.py:76
  44.9 19.3 %all-to-all-start.1 = ((f32[16,16,128]{2,1,0:T(8,128)}), f32[16,16,128]{2,1,0:T(8,128)S(1)}, u32[]{:S(2)}, u32[]{:S(2)}) async-start(f32[16,16,128]{2,1,0:T(8,128)} %reshape.71), calls=%async_computation.1 | async-start | bytes 262144 | tf_op jit(solution)/shard_map/all_to_all | solution.py:192
  66.5 24.2 %collective-permute-start.3 = (f32[20,64,128]{2,1,0:T(8,128)}, f32[20,64,128]{2,1,0:T(8,128)S(1)}, u32[]{:S(2)}, u32[]{:S(2)}) collective-permute-start(f32[20,64,128]{2,1,0:T(8,128)} %collective-permute-done), channel_id=1, source_target_pairs={{0,28},{4,0},{8,4},{12,8},{16,12},{20,16},{24,20},{28,24},{1,29},{... | collective-permute-start | bytes 1966088 | tf_op jit(solution)/shard_map/ppermute | solution.py:76
  70.1 18.6 %collective-permute-start.2 = (f32[20,64,128]{2,1,0:T(8,128)}, f32[20,64,128]{2,1,0:T(8,128)S(1)}, u32[]{:S(2)}, u32[]{:S(2)}) collective-permute-start(f32[20,64,128]{2,1,0:T(8,128)} %collective-permute-done.1), channel_id=1, source_target_pairs={{0,4},{4,8},{8,12},{12,16},{16,20},{20,24},{24,28},{28,0},{1,5},{5... | collective-permute-start | bytes 1966088 | tf_op jit(solution)/shard_map/ppermute | solution.py:75
  88.7 17.5 %collective-permute-start.4 = (f32[20,64,128]{2,1,0:T(8,128)S(1)}, f32[20,64,128]{2,1,0:T(8,128)S(1)}, u32[]{:S(2)}, u32[]{:S(2)}) collective-permute-start(f32[20,64,128]{2,1,0:T(8,128)S(1)} %collective-permute-done.2), channel_id=1, source_target_pairs={{0,4},{4,8},{8,12},{12,16},{16,20},{20,24},{24,28},{28,0},{1,5},{5... | collective-permute-start | bytes 1966088 | tf_op jit(solution)/shard_map/ppermute | solution.py:75
  90.7 17.5 %collective-permute-start.5 = (f32[20,64,128]{2,1,0:T(8,128)S(1)}, f32[20,64,128]{2,1,0:T(8,128)S(1)}, u32[]{:S(2)}, u32[]{:S(2)}) collective-permute-start(f32[20,64,128]{2,1,0:T(8,128)S(1)} %collective-permute-done.3), channel_id=1, source_target_pairs={{0,28},{4,0},{8,4},{12,8},{16,12},{20,16},{24,20},{28,24},{1,29},{... | collective-permute-start | bytes 1966088 | tf_op jit(solution)/shard_map/ppermute | solution.py:76
  106.2 9.5 %collective-permute-start.6 = (f32[10,64,128]{2,1,0:T(8,128)S(1)}, f32[10,64,128]{2,1,0:T(8,128)S(1)}, u32[]{:S(2)}, u32[]{:S(2)}) collective-permute-start(f32[10,64,128]{2,1,0:T(8,128)S(1)} %slice.592), channel_id=1, source_target_pairs={{0,4},{4,8},{8,12},{12,16},{16,20},{20,24},{24,28},{28,0},{1,5},{5... | collective-permute-start | bytes 983048 | tf_op jit(solution)/shard_map/ppermute | solution.py:83
  108.2 8.6 %collective-permute-start.7 = (f32[10,64,128]{2,1,0:T(8,128)S(1)}, f32[10,64,128]{2,1,0:T(8,128)S(1)}, u32[]{:S(2)}, u32[]{:S(2)}) collective-permute-start(f32[10,64,128]{2,1,0:T(8,128)S(1)} %slice.593), channel_id=1, source_target_pairs={{0,28},{4,0},{8,4},{12,8},{16,12},{20,16},{24,20},{28,24},{1,29},{... | collective-permute-start | bytes 983048 | tf_op jit(solution)/shard_map/ppermute | solution.py:84
  117.6 10.3 %collective-permute-start.9 = (f32[8,8,64,128]{3,2,1,0:T(8,128)}, f32[8,8,64,128]{3,2,1,0:T(8,128)}, u32[]{:S(2)}, u32[]{:S(2)}) collective-permute-start(f32[8,8,64,128]{3,2,1,0:T(8,128)} %get-tuple-element.57.own_ref), channel_id=1, source_target_pairs={{0,32},{32,0},{1,33},{33,1},{2,34},{34,2},{3,35},{35,3},{4,36},{36... | collective-permute-start | bytes 6291464 | tf_op jit(solution)/shard_map/ppermute | solution.py:160
  123.5 7.6 %collective-permute-start.8 = (f32[8,8,64,128]{3,2,1,0:T(8,128)}, f32[8,8,64,128]{3,2,1,0:T(8,128)}, u32[]{:S(2)}, u32[]{:S(2)}) collective-permute-start(f32[8,8,64,128]{3,2,1,0:T(8,128)} %get-tuple-element.58.own_ref), channel_id=1, source_target_pairs={{0,32},{32,0},{1,33},{33,1},{2,34},{34,2},{3,35},{35,3},{4,36},{36... | collective-permute-start | bytes 6291464 | tf_op jit(solution)/shard_map/ppermute | solution.py:160
  125.5 8.6 %collective-permute-start.11 = (f32[8,4,64,128]{3,2,1,0:T(8,128)S(1)}, f32[8,4,64,128]{3,2,1,0:T(8,128)}, u32[]{:S(2)}, u32[]{:S(2)}) collective-permute-start(f32[8,4,64,128]{3,2,1,0:T(8,128)S(1)} %fusion.55.own_ref), channel_id=1, source_target_pairs={{0,32},{32,0},{1,33},{33,1},{2,34},{34,2},{3,35},{35,3},{4,36},{36... | collective-permute-start | bytes 3145736 | tf_op jit(solution)/shard_map/ppermute | solution.py:160
  137.2 8.5 %collective-permute-start.10 = (f32[32,1024]{1,0:T(8,128)S(1)}, f32[32,1024]{1,0:T(8,128)S(1)}, u32[]{:S(2)}, u32[]{:S(2)}) collective-permute-start(f32[32,1024]{1,0:T(8,128)S(1)} %get-tuple-element.127), channel_id=1, source_target_pairs={{0,128},{1,129},{2,130},{3,131},{4,132},{5,133},{6,134},{7,135},{8... | collective-permute-start | bytes 393224 | tf_op jit(solution)/shard_map/ppermute | solution.py:200
  142.7 14.9 %collective-permute-start.14 = (f32[32,1024]{1,0:T(8,128)S(1)}, f32[32,1024]{1,0:T(8,128)S(1)}, u32[]{:S(2)}, u32[]{:S(2)}) collective-permute-start(f32[32,1024]{1,0:T(8,128)S(1)} %convolution_add_fusion.18), channel_id=1, source_target_pairs={{0,384},{1,385},{2,386},{3,387},{4,388},{5,389},{6,390},{7,391},{8... | collective-permute-start | bytes 393224 | tf_op jit(solution)/shard_map/ppermute | solution.py:200
  144.4 6.6 %collective-permute-start.12 = (f32[32,1536]{1,0:T(8,128)S(1)}, f32[32,1536]{1,0:T(8,128)S(1)}, u32[]{:S(2)}, u32[]{:S(2)}) collective-permute-start(f32[32,1536]{1,0:T(8,128)S(1)} %pad_maximum_fusion.2), channel_id=1, source_target_pairs={{0,256},{1,257},{2,258},{3,259},{4,260},{5,261},{6,262},{7,263},{8... | collective-permute-start | bytes 589832 | tf_op jit(solution)/shard_map/ppermute | solution.py:200
  149.6 2.3 %collective-permute-start.13 = (f32[32,1024]{1,0:T(8,128)S(1)}, f32[32,1024]{1,0:T(8,128)S(1)}, u32[]{:S(2)}, u32[]{:S(2)}) collective-permute-start(f32[32,1024]{1,0:T(8,128)S(1)} %get-tuple-element.128), channel_id=1, source_target_pairs={{128,256},{129,257},{130,258},{131,259},{132,260},{133,261},{134,2... | collective-permute-start | bytes 393224 | tf_op jit(solution)/shard_map/ppermute | solution.py:200
  150.3 5.5 %collective-permute-start.15 = (f32[32,1536]{1,0:T(8,128)S(1)}, f32[32,1536]{1,0:T(8,128)S(1)}, u32[]{:S(2)}, u32[]{:S(2)}) collective-permute-start(f32[32,1536]{1,0:T(8,128)S(1)} %pad_maximum_fusion.3), channel_id=1, source_target_pairs={{128,384},{129,385},{130,386},{131,387},{132,388},{133,389},{134,3... | collective-permute-start | bytes 589832 | tf_op jit(solution)/shard_map/ppermute | solution.py:200
  160.9 9.8 %collective-permute-start.19 = (f32[32,1024]{1,0:T(8,128)S(1)}, f32[32,1024]{1,0:T(8,128)S(1)}, u32[]{:S(2)}, u32[]{:S(2)}) collective-permute-start(f32[32,1024]{1,0:T(8,128)S(1)} %get-tuple-element.130), channel_id=1, source_target_pairs={{384,0},{385,1},{386,2},{387,3},{388,4},{389,5},{390,6},{391,7},{3... | collective-permute-start | bytes 393224 | tf_op jit(solution)/shard_map/ppermute | solution.py:200
  163.1 2.0 collective-permute-start.17
  164.4 7.3 %collective-permute-start.20 = (f32[32,1536]{1,0:T(8,128)S(1)}, f32[32,1536]{1,0:T(8,128)S(1)}, u32[]{:S(2)}, u32[]{:S(2)}) collective-permute-start(f32[32,1536]{1,0:T(8,128)S(1)} %pad_maximum_fusion.5), channel_id=1, source_target_pairs={{384,128},{385,129},{386,130},{387,131},{388,132},{389,133},{390,1... | collective-permute-start | bytes 589832 | tf_op jit(solution)/shard_map/ppermute | solution.py:200
  167.1 5.2 %collective-permute-start.21 = (f32[32,1024]{1,0:T(8,128)S(1)}, f32[32,1024]{1,0:T(8,128)S(1)}, u32[]{:S(2)}, u32[]{:S(2)}) collective-permute-start(f32[32,1024]{1,0:T(8,128)S(1)} %convolution_add_fusion.11), channel_id=1, source_target_pairs={{256,128},{257,129},{258,130},{259,131},{260,132},{261,133},{262,1... | collective-permute-start | bytes 393224 | tf_op jit(solution)/shard_map/ppermute | solution.py:200
  168.4 14.0 %collective-permute-start.18 = (f32[32,1536]{1,0:T(8,128)S(1)}, f32[32,1536]{1,0:T(8,128)S(1)}, u32[]{:S(2)}, u32[]{:S(2)}) collective-permute-start(f32[32,1536]{1,0:T(8,128)S(1)} %pad_maximum_fusion.4), channel_id=1, source_target_pairs={{256,0},{257,1},{258,2},{259,3},{260,4},{261,5},{262,6},{263,7},{2... | collective-permute-start | bytes 589832 | tf_op jit(solution)/shard_map/ppermute | solution.py:200
  174.3 12.7 %collective-permute-start.22 = (f32[32,1024]{1,0:T(8,128)S(1)}, f32[32,1024]{1,0:T(8,128)S(1)}, u32[]{:S(2)}, u32[]{:S(2)}) collective-permute-start(f32[32,1024]{1,0:T(8,128)S(1)} %convolution_add_fusion.9), channel_id=1, source_target_pairs={{128,0},{129,1},{130,2},{131,3},{132,4},{133,5},{134,6},{135,7},{1... | collective-permute-start | bytes 393224 | tf_op jit(solution)/shard_map/ppermute | solution.py:200
  (6 other events, 79.0 us)

commit v5 on v4

--- a/solution.py
+++ b/solution.py
@@ -158,10 +158,11 @@
     core = lax.axis_index("core").reshape(1).astype(jnp.int32)
     whole = pl.BlockSpec(memory_space=pltpu.VMEM)
     others = [lax.ppermute(part, "core", shift(2, 1)) for part in held]
-    found = []
-    for own, other in zip(held, others):
-        if found:
-            other, found[-1] = lax.optimization_barrier((other, found[-1]))
+
+    def lay(slot, after):
+        own, other = held[slot], others[slot]
+        if after is not None:
+            other, after = lax.optimization_barrier((other, after))
         shape = jax.ShapeDtypeStruct((own.shape[1], 2, share, 32 * k), jnp.bfloat16)
         both = pl.pallas_call(
             lay_out,
@@ -171,8 +172,9 @@
             compiler_params=pltpu.CompilerParams(vmem_limit_bytes=16 * 1024 * 1024),
             name="lay_out",
         )(core, own, other)
-        found.append(tuple(half.reshape(-1, 32 * k) for half in both))
-    return found, right
+        return tuple(half.reshape(-1, 32 * k) for half in both)
+
+    return lay, right
 
 
 def on_device(points, frequencies, phases, feature_weights, observed, factor):
@@ -192,7 +194,8 @@
         came = lax.all_to_all(send, ROW, 0, 0, tiled=True)
         return came.reshape(size, samples).T
 
-    (diagonal, beside, third), right = gather_blocks(factor, send, send_sides)
+    lay, right = gather_blocks(factor, send, send_sides)
+    diagonal = lay(0, None)
 
     here = lax.axis_index("x")
 
@@ -213,10 +216,13 @@
 
     first = times(right, diagonal, 1)
     near = move(first, 0, 1)
+    beside = lay(1, first)
+    third = lay(2, beside)
     skip = move(beyond(first), 0, 2)
-    far = move(times(first, beside, 1), 0, 3)
     second = times(right - times(near, beside, 1), diagonal, 1)
     near = move(second, 1, 2)
+    late, _ = lax.optimization_barrier((first, second))
+    far = move(times(late, beside, 1), 0, 3)
     skip_on = move(beyond(second), 1, 3)
     base = right - whole_third(skip)
     solved = times(base - times(near, beside, 1), diagonal, 1)

time: 211 us -> 207 us (0.981)
  waiting for transfers between devices: 38.7 us -> 42.6 us
  local copies, waits for them, and re-layouts: 25.9 us -> 22.3 us
  blocking collectives: 19.5 us -> 16.2 us
    all_to_all x1, waiting for transfers between devices: 2.52 us -> 10.2 us  [send_sides(): came = lax.all_to_all(send, ROW, 0, 0, tiled=True)]
    all_to_all x1, blocking collectives: 19.5 us -> 16.2 us  [on_device(): came = lax.all_to_all(send, ROW, 0, 0, tiled=True)]
    ppermute x3, waiting for transfers between devices: 20.3 us -> 17.5 us  [ring_gather(): up = lax.ppermute(up, axis, shift(size, 1))]
    ppermute x3, starting transfers between devices: 12 us -> 14.5 us  [ring_gather(): down = lax.ppermute(down, axis, shift(size, -1))]
  transfers between devices with their start and end apart: 25 -> 25, of which waited for: 9 -> 9; matrix products, arithmetic and copies ran while one was open for 27% -> 26% of each run, Pallas kernels for 3% -> 4%
where the time goes in v5:
time: 207 us; the launch traced here: 206 us
  starting transfers between devices  74 us (36%)
  waiting for transfers between devices  42.6 us (21%)
  matrix products  39.5 us (19%)
  local copies, waits for them, and re-layouts  22.3 us (11%)
  blocking collectives  16.2 us (8%)
  Pallas kernels  8.39 us (4%)
  other arithmetic  2.22 us (1%)
    ppermute x3, waiting for transfers between devices, ring_gather(): up = lax.ppermute(up, axis, shift(size, 1))  17.5 us
    all_to_all x1, blocking collectives, on_device(): came = lax.all_to_all(send, ROW, 0, 0, tiled=True)  16.2 us
    ppermute x3, starting transfers between devices, ring_gather(): down = lax.ppermute(down, axis, shift(size, -1))  14.5 us
    ppermute x12, starting transfers between devices, move(): return lax.ppermute(value, 'x', [(source, target)])  14.2 us
    all_to_all x1, starting transfers between devices, gather_blocks(): came = lax.all_to_all(send, ('x',) + Z, 0, 0, tiled=True)  13.7 us
    dot_general x24, matrix products, times(): lax.dot_general(jnp.concatenate([high, low], 0), right[0], dims, preferre...  12.9 us
    dot_general x24, matrix products, times(): lax.dot_general(high, right[1], dims, preferred_element_type=jnp.float32)  12.6 us
    dot_general x4, matrix products, feature_rows(): lax.dot_general(rows, frequencies * turn, (((0,), (0,)), ((), ())), preci...  12 us
  transfers between devices with their start and end apart: 25, of which 9 were waited for; matrix products, arithmetic and copies ran while one was open for 26% of the time, Pallas kernels for 4%

profile of v5, /device:TPU:1, one launch (start us, length us, event | category | flops | bytes accessed | tf_op | source)
XLA Modules:
  0.0 206.3 jit_solution(8097956700989500054)
XLA Ops:
  3.3 13.7 %all-to-all-start = ((f32[32,48,128]{2,1,0:T(8,128)}), f32[32,48,128]{2,1,0:T(8,128)S(1)}, u32[]{:S(2)}, u32[]{:S(2)}) async-start(f32[32,48,128]{2,1,0:T(8,128)} %bitcast.333), calls=%async_computation | async-start | bytes 1572864 | tf_op jit(solution)/shard_map/all_to_all | solution.py:147
  17.1 3.0 %add_convert_fusion.2 = bf16[64,8192]{1,0:T(8,128)(2,1)S(1)} fusion(f32[8,64]{1,0:T(8,128)S(1)} %bitcast.343, f32[8192]{0:T(1024)S(1)} %broadcast_multiply_fusion, f32[8,8192]{1,0:T(8,128)S(1)} %copy-done.5), kind=kOutput, calls=%fused_computation.18 | convolution fusion | flops 60358656 | bytes 1345536 | tf_op jit(solution)/shard_map/dot_general | solution.py:43
  20.1 3.0 %add_convert_fusion.1 = bf16[64,8192]{1,0:T(8,128)(2,1)S(1)} fusion(f32[8,64]{1,0:T(8,128)S(1)} %bitcast.342, f32[8192]{0:T(1024)S(1)} %broadcast_multiply_fusion, f32[8,8192]{1,0:T(8,128)S(1)} %copy-done.5), kind=kOutput, calls=%fused_computation.17 | convolution fusion | flops 60358656 | bytes 1345536 | tf_op jit(solution)/shard_map/dot_general | solution.py:43
  24.3 3.0 %add_convert_fusion = bf16[64,8192]{1,0:T(8,128)(2,1)S(1)} fusion(f32[8,64]{1,0:T(8,128)S(1)} %bitcast.341, f32[8192]{0:T(1024)S(1)} %broadcast_multiply_fusion, f32[8,8192]{1,0:T(8,128)S(1)} %copy-done.5), kind=kOutput, calls=%fused_computation.16 | convolution fusion | flops 60358656 | bytes 1345536 | tf_op jit(solution)/shard_map/dot_general | solution.py:43
  27.9 3.0 %add_convert_fusion.3 = bf16[64,8192]{1,0:T(8,128)(2,1)S(1)} fusion(f32[8,64]{1,0:T(8,128)S(1)} %bitcast.340, f32[8192]{0:T(1024)S(1)} %broadcast_multiply_fusion, f32[8,8192]{1,0:T(8,128)S(1)} %copy-done.5), kind=kOutput, calls=%fused_computation.19 | convolution fusion | flops 60358656 | bytes 1345536 | tf_op jit(solution)/shard_map/dot_general | solution.py:43
  37.1 5.1 %collective-permute-start = (f32[20,64,128]{2,1,0:T(8,128)S(1)}, f32[20,64,128]{2,1,0:T(8,128)}, u32[]{:S(2)}, u32[]{:S(2)}) collective-permute-start(f32[20,64,128]{2,1,0:T(8,128)S(1)} %pad_maximum_fusion), channel_id=1, source_target_pairs={{0,28},{4,0},{8,4},{12,8},{16,12},{20,16},{24,20},{28,24},{1,29},{... | collective-permute-start | bytes 1966088 | tf_op jit(solution)/shard_map/ppermute | solution.py:76
  42.2 1.9 collective-permute-start.1
  44.1 9.2 %all-to-all-start.1 = ((f32[16,16,128]{2,1,0:T(8,128)}), f32[16,16,128]{2,1,0:T(8,128)S(1)}, u32[]{:S(2)}, u32[]{:S(2)}) async-start(f32[16,16,128]{2,1,0:T(8,128)} %reshape.71), calls=%async_computation.1 | async-start | bytes 262144 | tf_op jit(solution)/shard_map/all_to_all | solution.py:194
  53.3 10.2 %all-to-all-done.1 = f32[16,16,128]{2,1,0:T(8,128)S(1)} async-done(((f32[16,16,128]{2,1,0:T(8,128)}), f32[16,16,128]{2,1,0:T(8,128)S(1)}, u32[]{:S(2)}, u32[]{:S(2)}) %all-to-all-start.1) | async-done | bytes 131104 | tf_op jit(solution)/shard_map/all_to_all | solution.py:194
  63.8 4.9 %collective-permute-start.3 = (f32[20,64,128]{2,1,0:T(8,128)}, f32[20,64,128]{2,1,0:T(8,128)S(1)}, u32[]{:S(2)}, u32[]{:S(2)}) collective-permute-start(f32[20,64,128]{2,1,0:T(8,128)} %collective-permute-done), channel_id=1, source_target_pairs={{0,28},{4,0},{8,4},{12,8},{16,12},{20,16},{24,20},{28,24},{1,29},{... | collective-permute-start | bytes 1966088 | tf_op jit(solution)/shard_map/ppermute | solution.py:76
  77.2 10.1 %collective-permute-done.2 = f32[20,64,128]{2,1,0:T(8,128)S(1)} collective-permute-done((f32[20,64,128]{2,1,0:T(8,128)}, f32[20,64,128]{2,1,0:T(8,128)S(1)}, u32[]{:S(2)}, u32[]{:S(2)}) %collective-permute-start.2) | collective-permute-done | bytes 655392 | tf_op jit(solution)/shard_map/ppermute | solution.py:75
  89.2 4.6 %collective-permute-start.5 = (f32[20,64,128]{2,1,0:T(8,128)S(1)}, f32[20,64,128]{2,1,0:T(8,128)S(1)}, u32[]{:S(2)}, u32[]{:S(2)}) collective-permute-start(f32[20,64,128]{2,1,0:T(8,128)S(1)} %collective-permute-done.3), channel_id=1, source_target_pairs={{0,28},{4,0},{8,4},{12,8},{16,12},{20,16},{24,20},{28,24},{1,29},{... | collective-permute-start | bytes 1966088 | tf_op jit(solution)/shard_map/ppermute | solution.py:76
  97.4 7.4 %collective-permute-done.4 = f32[20,64,128]{2,1,0:T(8,128)S(1)} collective-permute-done((f32[20,64,128]{2,1,0:T(8,128)S(1)}, f32[20,64,128]{2,1,0:T(8,128)S(1)}, u32[]{:S(2)}, u32[]{:S(2)}) %collective-permute-start.4) | collective-permute-done | bytes 655392 | tf_op jit(solution)/shard_map/ppermute | solution.py:75
  104.8 1.9 collective-permute-start.6
  106.7 4.6 %collective-permute-start.9 = (f32[10,64,128]{2,1,0:T(8,128)S(1)}, f32[10,64,128]{2,1,0:T(8,128)S(1)}, u32[]{:S(2)}, u32[]{:S(2)}) collective-permute-start(f32[10,64,128]{2,1,0:T(8,128)S(1)} %slice.601), channel_id=1, source_target_pairs={{0,28},{4,0},{8,4},{12,8},{16,12},{20,16},{24,20},{28,24},{1,29},{... | collective-permute-start | bytes 983048 | tf_op jit(solution)/shard_map/ppermute | solution.py:84
  116.2 5.8 %collective-permute-start.7 = (f32[8,8,64,128]{3,2,1,0:T(8,128)}, f32[8,8,64,128]{3,2,1,0:T(8,128)}, u32[]{:S(2)}, u32[]{:S(2)}) collective-permute-start(f32[8,8,64,128]{3,2,1,0:T(8,128)} %get-tuple-element.52.own_ref), channel_id=1, source_target_pairs={{0,32},{32,0},{1,33},{33,1},{2,34},{34,2},{3,35},{35,3},{4,36},{36... | collective-permute-start | bytes 6291464 | tf_op jit(solution)/shard_map/ppermute | solution.py:160
  124.9 1.9 collective-permute-start.10
  126.9 2.4 %collective-permute-start.11 = (f32[8,4,64,128]{3,2,1,0:T(8,128)S(1)}, f32[8,4,64,128]{3,2,1,0:T(8,128)}, u32[]{:S(2)}, u32[]{:S(2)}) collective-permute-start(f32[8,4,64,128]{3,2,1,0:T(8,128)S(1)} %fusion.56.own_ref), channel_id=1, source_target_pairs={{0,32},{32,0},{1,33},{33,1},{2,34},{34,2},{3,35},{35,3},{4,36},{36... | collective-permute-start | bytes 3145736 | tf_op jit(solution)/shard_map/ppermute | solution.py:160
  129.4 3.0 %lay_out.3 = (bf16[8,2,64,1024]{3,2,1,0:T(8,128)(2,1)S(1)}, bf16[8,2,64,1024]{3,2,1,0:T(8,128)(2,1)S(1)}) custom-call(s32[1]{0:T(128)} %bitcast.43.core_ref, f32[8,8,64,128]{3,2,1,0:T(8,128)} %get-tuple-element.52.own_ref, f32[8,8,64,128]{3,2,1,0:T(8,128)} %collective-permute-done.7.other_ref), custom_call_target="tpu_custom_call" | custom-call | tf_op jit(solution)/shard_map/lay_out/pallas_call | solution.py:167
  134.0 3.5 %collective-permute-start.8 = (f32[32,1024]{1,0:T(8,128)S(1)}, f32[32,1024]{1,0:T(8,128)S(1)}, u32[]{:S(2)}, u32[]{:S(2)}) collective-permute-start(f32[32,1024]{1,0:T(8,128)S(1)} %get-tuple-element.30), channel_id=1, source_target_pairs={{0,128},{1,129},{2,130},{3,131},{4,132},{5,133},{6,134},{7,135},{8... | collective-permute-start | bytes 393224 | tf_op jit(solution)/shard_map/ppermute | solution.py:203
  137.5 3.0 %lay_out.4 = (bf16[8,2,64,1024]{3,2,1,0:T(8,128)(2,1)S(1)}, bf16[8,2,64,1024]{3,2,1,0:T(8,128)(2,1)S(1)}) custom-call(s32[1]{0:T(128)} %bitcast.43.core_ref, f32[8,8,64,128]{3,2,1,0:T(8,128)} %get-tuple-element.51.own_ref, f32[8,8,64,128]{3,2,1,0:T(8,128)} %collective-permute-done.10.other_ref), custom_call_target="tpu_custom_call" | custom-call | tf_op jit(solution)/shard_map/lay_out/pallas_call | solution.py:167
  176.3 7.3 %collective-permute-done.18 = f32[32,1536]{1,0:T(8,128)S(1)} collective-permute-done((f32[32,1536]{1,0:T(8,128)S(1)}, f32[32,1536]{1,0:T(8,128)S(1)}, u32[]{:S(2)}, u32[]{:S(2)}) %collective-permute-start.18) | collective-permute-done | bytes 196640 | tf_op jit(solution)/shard_map/ppermute | solution.py:203
  184.2 2.9 %collective-permute-done.22 = f32[32,1024]{1,0:T(8,128)S(1)} collective-permute-done((f32[32,1024]{1,0:T(8,128)S(1)}, f32[32,1024]{1,0:T(8,128)S(1)}, u32[]{:S(2)}, u32[]{:S(2)}) %collective-permute-start.22) | collective-permute-done | bytes 131104 | tf_op jit(solution)/shard_map/ppermute | solution.py:203
  189.0 16.2 %all_to_all.15 = f32[16,16,128]{2,1,0:T(8,128)S(1)} all-to-all(f32[16,16,128]{2,1,0:T(8,128)S(1)} %reshape.80), channel_id=1, replica_groups=mesh['x'=4,'zh'=2,'core'=2,'y'=8,'zl'=4] {'x','zh','core'}, dimensions={0} | all-to-all | bytes 262144 | tf_op jit(solution)/shard_map/all_to_all | solution.py:248
  (168 shorter events, 73.8 us)
Async XLA Ops:
  3.3 33.0 %all-to-all-start = ((f32[32,48,128]{2,1,0:T(8,128)}), f32[32,48,128]{2,1,0:T(8,128)S(1)}, u32[]{:S(2)}, u32[]{:S(2)}) async-start(f32[32,48,128]{2,1,0:T(8,128)} %bitcast.333), calls=%async_computation | async-start | bytes 1572864 | tf_op jit(solution)/shard_map/all_to_all | solution.py:147
  37.1 26.7 %collective-permute-start = (f32[20,64,128]{2,1,0:T(8,128)S(1)}, f32[20,64,128]{2,1,0:T(8,128)}, u32[]{:S(2)}, u32[]{:S(2)}) collective-permute-start(f32[20,64,128]{2,1,0:T(8,128)S(1)} %pad_maximum_fusion), channel_id=1, source_target_pairs={{0,28},{4,0},{8,4},{12,8},{16,12},{20,16},{24,20},{28,24},{1,29},{... | collective-permute-start | bytes 1966088 | tf_op jit(solution)/shard_map/ppermute | solution.py:76
  42.2 26.5 %collective-permute-start.1 = (f32[20,64,128]{2,1,0:T(8,128)S(1)}, f32[20,64,128]{2,1,0:T(8,128)}, u32[]{:S(2)}, u32[]{:S(2)}) collective-permute-start(f32[20,64,128]{2,1,0:T(8,128)S(1)} %pad_maximum_fusion), channel_id=1, source_target_pairs={{0,4},{4,8},{8,12},{12,16},{16,20},{20,24},{24,28},{28,0},{1,5},{5... | collective-permute-start | bytes 1966088 | tf_op jit(solution)/shard_map/ppermute | solution.py:75
  44.1 19.3 %all-to-all-start.1 = ((f32[16,16,128]{2,1,0:T(8,128)}), f32[16,16,128]{2,1,0:T(8,128)S(1)}, u32[]{:S(2)}, u32[]{:S(2)}) async-start(f32[16,16,128]{2,1,0:T(8,128)} %reshape.71), calls=%async_computation.1 | async-start | bytes 262144 | tf_op jit(solution)/shard_map/all_to_all | solution.py:194
  63.8 25.4 %collective-permute-start.3 = (f32[20,64,128]{2,1,0:T(8,128)}, f32[20,64,128]{2,1,0:T(8,128)S(1)}, u32[]{:S(2)}, u32[]{:S(2)}) collective-permute-start(f32[20,64,128]{2,1,0:T(8,128)} %collective-permute-done), channel_id=1, source_target_pairs={{0,28},{4,0},{8,4},{12,8},{16,12},{20,16},{24,20},{28,24},{1,29},{... | collective-permute-start | bytes 1966088 | tf_op jit(solution)/shard_map/ppermute | solution.py:76
  68.7 18.6 %collective-permute-start.2 = (f32[20,64,128]{2,1,0:T(8,128)}, f32[20,64,128]{2,1,0:T(8,128)S(1)}, u32[]{:S(2)}, u32[]{:S(2)}) collective-permute-start(f32[20,64,128]{2,1,0:T(8,128)} %collective-permute-done.1), channel_id=1, source_target_pairs={{0,4},{4,8},{8,12},{12,16},{16,20},{20,24},{24,28},{28,0},{1,5},{5... | collective-permute-start | bytes 1966088 | tf_op jit(solution)/shard_map/ppermute | solution.py:75
  87.3 17.5 %collective-permute-start.4 = (f32[20,64,128]{2,1,0:T(8,128)S(1)}, f32[20,64,128]{2,1,0:T(8,128)S(1)}, u32[]{:S(2)}, u32[]{:S(2)}) collective-permute-start(f32[20,64,128]{2,1,0:T(8,128)S(1)} %collective-permute-done.2), channel_id=1, source_target_pairs={{0,4},{4,8},{8,12},{12,16},{16,20},{20,24},{24,28},{28,0},{1,5},{5... | collective-permute-start | bytes 1966088 | tf_op jit(solution)/shard_map/ppermute | solution.py:75
  89.2 17.5 %collective-permute-start.5 = (f32[20,64,128]{2,1,0:T(8,128)S(1)}, f32[20,64,128]{2,1,0:T(8,128)S(1)}, u32[]{:S(2)}, u32[]{:S(2)}) collective-permute-start(f32[20,64,128]{2,1,0:T(8,128)S(1)} %collective-permute-done.3), channel_id=1, source_target_pairs={{0,28},{4,0},{8,4},{12,8},{16,12},{20,16},{24,20},{28,24},{1,29},{... | collective-permute-start | bytes 1966088 | tf_op jit(solution)/shard_map/ppermute | solution.py:76
  104.8 9.5 %collective-permute-start.6 = (f32[10,64,128]{2,1,0:T(8,128)S(1)}, f32[10,64,128]{2,1,0:T(8,128)S(1)}, u32[]{:S(2)}, u32[]{:S(2)}) collective-permute-start(f32[10,64,128]{2,1,0:T(8,128)S(1)} %slice.592), channel_id=1, source_target_pairs={{0,4},{4,8},{8,12},{12,16},{16,20},{20,24},{24,28},{28,0},{1,5},{5... | collective-permute-start | bytes 983048 | tf_op jit(solution)/shard_map/ppermute | solution.py:83
  106.7 8.6 %collective-permute-start.9 = (f32[10,64,128]{2,1,0:T(8,128)S(1)}, f32[10,64,128]{2,1,0:T(8,128)S(1)}, u32[]{:S(2)}, u32[]{:S(2)}) collective-permute-start(f32[10,64,128]{2,1,0:T(8,128)S(1)} %slice.601), channel_id=1, source_target_pairs={{0,28},{4,0},{8,4},{12,8},{16,12},{20,16},{24,20},{28,24},{1,29},{... | collective-permute-start | bytes 983048 | tf_op jit(solution)/shard_map/ppermute | solution.py:84
  116.2 13.2 %collective-permute-start.7 = (f32[8,8,64,128]{3,2,1,0:T(8,128)}, f32[8,8,64,128]{3,2,1,0:T(8,128)}, u32[]{:S(2)}, u32[]{:S(2)}) collective-permute-start(f32[8,8,64,128]{3,2,1,0:T(8,128)} %get-tuple-element.52.own_ref), channel_id=1, source_target_pairs={{0,32},{32,0},{1,33},{33,1},{2,34},{34,2},{3,35},{35,3},{4,36},{36... | collective-permute-start | bytes 6291464 | tf_op jit(solution)/shard_map/ppermute | solution.py:160
  124.9 12.6 %collective-permute-start.10 = (f32[8,8,64,128]{3,2,1,0:T(8,128)}, f32[8,8,64,128]{3,2,1,0:T(8,128)}, u32[]{:S(2)}, u32[]{:S(2)}) collective-permute-start(f32[8,8,64,128]{3,2,1,0:T(8,128)} %get-tuple-element.51.own_ref), channel_id=1, source_target_pairs={{0,32},{32,0},{1,33},{33,1},{2,34},{34,2},{3,35},{35,3},{4,36},{36... | collective-permute-start | bytes 6291464 | tf_op jit(solution)/shard_map/ppermute | solution.py:160
  126.9 13.6 %collective-permute-start.11 = (f32[8,4,64,128]{3,2,1,0:T(8,128)S(1)}, f32[8,4,64,128]{3,2,1,0:T(8,128)}, u32[]{:S(2)}, u32[]{:S(2)}) collective-permute-start(f32[8,4,64,128]{3,2,1,0:T(8,128)S(1)} %fusion.56.own_ref), channel_id=1, source_target_pairs={{0,32},{32,0},{1,33},{33,1},{2,34},{34,2},{3,35},{35,3},{4,36},{36... | collective-permute-start | bytes 3145736 | tf_op jit(solution)/shard_map/ppermute | solution.py:160
  134.0 10.4 %collective-permute-start.8 = (f32[32,1024]{1,0:T(8,128)S(1)}, f32[32,1024]{1,0:T(8,128)S(1)}, u32[]{:S(2)}, u32[]{:S(2)}) collective-permute-start(f32[32,1024]{1,0:T(8,128)S(1)} %get-tuple-element.30), channel_id=1, source_target_pairs={{0,128},{1,129},{2,130},{3,131},{4,132},{5,133},{6,134},{7,135},{8... | collective-permute-start | bytes 393224 | tf_op jit(solution)/shard_map/ppermute | solution.py:203
  143.1 9.4 %collective-permute-start.12 = (f32[32,1536]{1,0:T(8,128)S(1)}, f32[32,1536]{1,0:T(8,128)S(1)}, u32[]{:S(2)}, u32[]{:S(2)}) collective-permute-start(f32[32,1536]{1,0:T(8,128)S(1)} %pad_maximum_fusion.2), channel_id=1, source_target_pairs={{0,256},{1,257},{2,258},{3,259},{4,260},{5,261},{6,262},{7,263},{8... | collective-permute-start | bytes 589832 | tf_op jit(solution)/shard_map/ppermute | solution.py:203
  147.4 6.0 %collective-permute-start.13 = (f32[32,1024]{1,0:T(8,128)S(1)}, f32[32,1024]{1,0:T(8,128)S(1)}, u32[]{:S(2)}, u32[]{:S(2)}) collective-permute-start(f32[32,1024]{1,0:T(8,128)S(1)} %get-tuple-element.124), channel_id=1, source_target_pairs={{128,256},{129,257},{130,258},{131,259},{132,260},{133,261},{134,2... | collective-permute-start | bytes 393224 | tf_op jit(solution)/shard_map/ppermute | solution.py:203
  150.5 8.6 %collective-permute-start.14 = (f32[32,1024]{1,0:T(8,128)S(1)}, f32[32,1024]{1,0:T(8,128)S(1)}, u32[]{:S(2)}, u32[]{:S(2)}) collective-permute-start(f32[32,1024]{1,0:T(8,128)S(1)} %convolution_add_fusion.18), channel_id=1, source_target_pairs={{0,384},{1,385},{2,386},{3,387},{4,388},{5,389},{6,390},{7,391},{8... | collective-permute-start | bytes 393224 | tf_op jit(solution)/shard_map/ppermute | solution.py:203
  151.8 5.5 %collective-permute-start.15 = (f32[32,1536]{1,0:T(8,128)S(1)}, f32[32,1536]{1,0:T(8,128)S(1)}, u32[]{:S(2)}, u32[]{:S(2)}) collective-permute-start(f32[32,1536]{1,0:T(8,128)S(1)} %pad_maximum_fusion.3), channel_id=1, source_target_pairs={{128,384},{129,385},{130,386},{131,387},{132,388},{133,389},{134,3... | collective-permute-start | bytes 589832 | tf_op jit(solution)/shard_map/ppermute | solution.py:203
  162.3 9.5 %collective-permute-start.19 = (f32[32,1024]{1,0:T(8,128)S(1)}, f32[32,1024]{1,0:T(8,128)S(1)}, u32[]{:S(2)}, u32[]{:S(2)}) collective-permute-start(f32[32,1024]{1,0:T(8,128)S(1)} %get-tuple-element.126), channel_id=1, source_target_pairs={{384,0},{385,1},{386,2},{387,3},{388,4},{389,5},{390,6},{391,7},{3... | collective-permute-start | bytes 393224 | tf_op jit(solution)/shard_map/ppermute | solution.py:203
  164.6 2.0 collective-permute-start.17
  165.9 6.5 %collective-permute-start.20 = (f32[32,1536]{1,0:T(8,128)S(1)}, f32[32,1536]{1,0:T(8,128)S(1)}, u32[]{:S(2)}, u32[]{:S(2)}) collective-permute-start(f32[32,1536]{1,0:T(8,128)S(1)} %pad_maximum_fusion.5), channel_id=1, source_target_pairs={{384,128},{385,129},{386,130},{387,131},{388,132},{389,133},{390,1... | collective-permute-start | bytes 589832 | tf_op jit(solution)/shard_map/ppermute | solution.py:203
  168.6 4.1 %collective-permute-start.21 = (f32[32,1024]{1,0:T(8,128)S(1)}, f32[32,1024]{1,0:T(8,128)S(1)}, u32[]{:S(2)}, u32[]{:S(2)}) collective-permute-start(f32[32,1024]{1,0:T(8,128)S(1)} %convolution_add_fusion.11), channel_id=1, source_target_pairs={{256,128},{257,129},{258,130},{259,131},{260,132},{261,133},{262,1... | collective-permute-start | bytes 393224 | tf_op jit(solution)/shard_map/ppermute | solution.py:203
  169.9 13.6 %collective-permute-start.18 = (f32[32,1536]{1,0:T(8,128)S(1)}, f32[32,1536]{1,0:T(8,128)S(1)}, u32[]{:S(2)}, u32[]{:S(2)}) collective-permute-start(f32[32,1536]{1,0:T(8,128)S(1)} %pad_maximum_fusion.4), channel_id=1, source_target_pairs={{256,0},{257,1},{258,2},{259,3},{260,4},{261,5},{262,6},{263,7},{2... | collective-permute-start | bytes 589832 | tf_op jit(solution)/shard_map/ppermute | solution.py:203
  175.0 12.1 %collective-permute-start.22 = (f32[32,1024]{1,0:T(8,128)S(1)}, f32[32,1024]{1,0:T(8,128)S(1)}, u32[]{:S(2)}, u32[]{:S(2)}) collective-permute-start(f32[32,1024]{1,0:T(8,128)S(1)} %convolution_add_fusion.9), channel_id=1, source_target_pairs={{128,0},{129,1},{130,2},{131,3},{132,4},{133,5},{134,6},{135,7},{1... | collective-permute-start | bytes 393224 | tf_op jit(solution)/shard_map/ppermute | solution.py:203
  (7 other events, 116.5 us)
